TPU v7x, 256 devices: a whole 4x4x8 slice. The times are simulated.
256 devices in a mesh: axial: 128 (over x, z_lo, y, core), radial: 2 (over z_hi).
Axes of the slice: x: 4, y: 4, z: 8 (z_hi: 2, z_lo: 4; z = z_hi * 4 + z_lo), core: 2. Of those that a mesh axis runs over, the one named last changes fastest.
Arguments:
- parcel_load: float32 [5, 4194304], P(None, ('axial', 'radial')), may hold values from -6 to 6
- parcel_offset: float32 [3, 4194304], P(None, ('axial', 'radial')), may hold values from 0 to 1
- parcel_cell: int32 [4194304], P(('axial', 'radial')), may hold values from 0 to 63
- cross_rows: int32 [2, 2097152], P(None, ('axial', 'radial')), may hold values from -1 to 16383, as said below
- block_brick: int32 [65536], P(('axial', 'radial')), may hold values from 0 to 1023
- gas: float32 [5, 512, 128, 256], P(None, 'axial', 'radial'), may hold values from -6 to 6
Outputs:
- source: float32 [5, 512, 128, 256], P(None, 'axial', 'radial')
- parcel_gas: bfloat16 [5, 8388608], P(None, ('axial', 'radial'))
Inputs may be any that keep to these rules, and one draw needn't show every extreme that they name: `cross_rows`: on each half slab the non-empty entries of a list come first, and all rows named in both lists are distinct; the upward lists of some half slabs are full with 8192 rows in every draw.
All inputs are finite; a program needn't handle non-finite values.
Results may differ from a plain program's by a relative error of at most 0.001.
Values sent between devices are 32-bit elements; how exact they have to be, the bound alone decides.
A program may use at most 64 MiB of HBM per device.

v0:
```python
import functools

import jax
import jax.numpy as jnp
from jax import lax
from jax.experimental import pallas as pl
from jax.experimental.pallas import tpu as pltpu
from jax.sharding import PartitionSpec as P

COUPLE = 0.5
LANES = 128
TILE = 256
FIELDS = 5
GROUP = 6
SPAN = 4 * GROUP
NT = (((1,), (1,)), ((), ()))
F32 = jnp.float32
BF16 = jnp.bfloat16


def split(x):
    high = x.astype(BF16).astype(F32)
    return high, x - high


def hat(x):
    return jnp.maximum(1.0 - jnp.abs(x), 0.0)


def row_numbers(shape):
    return lax.broadcasted_iota(jnp.int32, shape, 0)


def gather_kernel(load, offset, cell, rows, up, down, stay, table, base, corner, gone):
    count = load.shape[1]
    blocks = count // LANES
    slots = rows.shape[1]
    axis_row = row_numbers((3, count))
    coords = lax.shift_right_logical(
        jnp.broadcast_to(cell[...], (3, count)), 4 - 2 * axis_row
    ) & 3
    corner[...] = jnp.concatenate([jnp.zeros((5, count), F32), coords.astype(F32)], 0)
    base[...] = jnp.concatenate([load[...], offset[...]], 0)

    def fill(step, carry):
        at = pl.multiple_of(step * 2 * LANES, 2 * LANES)
        pair = base[:, pl.ds(at, 2 * LANES)] + corner[:, pl.ds(at, 2 * LANES)]
        both = jnp.concatenate([pair[:, :LANES], pair[:, LANES:]], 0)
        high, low = split(both)
        place = pl.multiple_of(step * 16, 16)
        table[pl.ds(place, 16), :] = jnp.concatenate([high, low], 1).astype(BF16)
        return carry

    lax.fori_loop(0, blocks // 2, fill, 0, unroll=8)
    gone[...] = jnp.zeros_like(gone)

    for side, out in ((0, up), (1, down)):
        out[...] = jnp.zeros_like(out)
        named = jnp.sum((rows[side : side + 1, :] >= 0).astype(F32)).astype(jnp.int32)

        def tile_step(step, carry, side=side, out=out):
            at = pl.multiple_of(step * TILE, TILE)
            row = rows[side : side + 1, pl.ds(at, TILE)]
            lane = row & (LANES - 1)
            block = lax.shift_right_arithmetic(row, 7)
            number = row_numbers((LANES, TILE))
            lane_hot = jnp.where(number == lane, 1.0, 0.0).astype(BF16)
            block_hot = jnp.where(number == block, 1.0, 0.0).astype(BF16)
            gone[...] += lax.dot_general(block_hot, lane_hot, NT, preferred_element_type=F32)
            wanted = jnp.concatenate([lane_hot, lane_hot], 0)
            block8 = jnp.broadcast_to(block, (8, TILE))
            found = jnp.zeros((8, TILE), F32)
            for chunk in range(blocks // 16):
                part = jnp.dot(
                    table[chunk * 128 : chunk * 128 + 128, :], wanted,
                    preferred_element_type=F32,
                )
                for i in range(16):
                    found = jnp.where(
                        block8 == chunk * 16 + i, part[8 * i : 8 * i + 8, :], found
                    )
            out[:, pl.ds(at, TILE)] = found
            return carry

        lax.fori_loop(0, (named + TILE - 1) // TILE, tile_step, 0)

    def keep(step, carry):
        at = pl.multiple_of(step * LANES, LANES)
        left = 1.0 - gone[pl.ds(step, 1), :]
        stay[:, pl.ds(at, LANES)] = (
            base[:, pl.ds(at, LANES)] * left + corner[:, pl.ds(at, LANES)]
        )
        return carry

    lax.fori_loop(0, blocks, keep, 0, unroll=8)


def gather_call(load, offset, cell, rows):
    count = load.shape[1]
    slots = rows.shape[1]
    moved = jax.ShapeDtypeStruct((8, slots), F32)
    return pl.pallas_call(
        gather_kernel,
        out_shape=(moved, moved, jax.ShapeDtypeStruct((8, count), F32)),
        scratch_shapes=[
            pltpu.VMEM((8 * (count // LANES), 2 * LANES), BF16),
            pltpu.VMEM((8, count), F32),
            pltpu.VMEM((8, count), F32),
            pltpu.VMEM((count // LANES, LANES), F32),
        ],
        compiler_params=pltpu.CompilerParams(vmem_limit_bytes=24 * 2**20),
        name="gather_rows",
    )(load, offset, cell.reshape(1, count), rows)


class Grid:
    def __init__(self, span_y, span_z):
        self.span_y = span_y
        self.span_z = span_z
        self.per_row = span_z // 4
        self.bricks_y = span_y // 4
        self.groups = -(-self.bricks_y // GROUP)
        self.rows_z = span_z + 8
        self.rows = self.groups * FIELDS * self.rows_z
        self.pad_y = self.groups * SPAN

    def place(self, brick):
        z = brick % self.per_row
        y = (brick // self.per_row) % self.bricks_y
        group = y // GROUP
        first = group * (FIELDS * self.rows_z) + 4 * z
        return first, (4 * (y - group * GROUP)).astype(F32)


def plane_weights(block, shift_y):
    number = row_numbers((8, LANES)).astype(F32)
    x = hat(number - block[5:6])
    y = block[6:7] + shift_y
    parts = [hat(number + 8.0 * k - y) for k in range(SPAN // 8)]
    last = hat(float(SPAN) - y)
    pieces = [x[i : i + 1] * part for i in range(5) for part in parts]
    return split(jnp.concatenate(pieces + [x * last], 0))


def depth_weights(block):
    return hat(row_numbers((8, LANES)).astype(F32) - block[7:8])


def doubled(x):
    high, low = split(x)
    both = jnp.concatenate([high, low], 0).astype(BF16)
    return jnp.concatenate([both, both], 1)


def deposit_block(grid, block, brick, total):
    first, shift_y = grid.place(brick)
    high, low = plane_weights(block, shift_y)
    plane = jnp.concatenate([high.astype(BF16), low.astype(BF16)], 1)
    depth = depth_weights(block)
    loads = jnp.concatenate([block[f : f + 1] * depth for f in range(FIELDS)], 0)
    both = lax.dot_general(doubled(loads), plane, NT, preferred_element_type=F32)
    summed = both[: 8 * FIELDS] + both[8 * FIELDS :]
    for f in range(FIELDS):
        rows = pl.ds(first + f * grid.rows_z, 8)
        total[rows, :] += summed[8 * f : 8 * f + 8]


def sample_block(grid, block, brick, held):
    first, shift_y = grid.place(brick)
    high, low = plane_weights(block, shift_y)
    plane = jnp.concatenate([high.astype(BF16), low.astype(BF16)], 0)
    fields = jnp.concatenate(
        [held[pl.ds(first + f * grid.rows_z, 8), :] for f in range(FIELDS)], 0
    )
    both = jnp.dot(doubled(fields), plane, preferred_element_type=F32)
    summed = both[: 8 * FIELDS] + both[8 * FIELDS :]
    depth = depth_weights(block)
    return jnp.concatenate(
        [
            jnp.sum(summed[8 * f : 8 * f + 8] * depth, axis=0, keepdims=True)
            for f in range(FIELDS)
        ],
        0,
    )


UNROLL = 4


def deposit_loop(grid, parcels, bricks, offset, count, total):
    def step(turn, carry):
        for i in range(UNROLL):
            at = turn * UNROLL + i
            block = parcels[:, pl.ds(pl.multiple_of(at * LANES, LANES), LANES)]
            deposit_block(grid, block, bricks[offset + at], total)
        return carry

    lax.fori_loop(0, count // UNROLL, step, 0)


def deposit_stay_kernel(grid, bricks, parcels, total):
    total[...] = jnp.zeros_like(total)
    deposit_loop(grid, parcels, bricks, 0, parcels.shape[1] // LANES, total)


def deposit_moved_kernel(
    grid, bricks, place, lower, upper, held, gas, sums, up, down, row, total
):
    total[...] = held[...]
    blocks = lower.shape[1] // LANES
    start = bricks.shape[0] - 2 * blocks
    deposit_loop(grid, lower, bricks, start, blocks, total)
    deposit_loop(grid, upper, bricks, start + blocks, blocks, total)
    picked = row_numbers((160, LANES))
    lane = lax.broadcasted_iota(jnp.int32, (160, LANES), 1)
    edge = picked - 5 * SPAN
    wanted = jnp.where(
        picked < 5 * SPAN, picked, jnp.where(edge % 8 == 0, 5 * SPAN + edge // 8, -1)
    )
    select = jnp.where(lane == wanted, 1.0, 0.0).astype(BF16)
    select = jnp.concatenate([select, select], 1)
    for f in range(FIELDS):
        carried = None
        for group in range(grid.groups):
            first = (group * FIELDS + f) * grid.rows_z
            high, low = split(total[first : first + grid.span_z, :])
            both = jnp.concatenate([high.astype(BF16), low.astype(BF16)], 1)
            turned = lax.dot_general(select, both, NT, preferred_element_type=F32)
            for x in range(5):
                piece = turned[x * SPAN : (x + 1) * SPAN]
                if carried is not None:
                    head = piece[:8] + carried[8 * x : 8 * x + 8]
                    piece = jnp.concatenate([head, piece[8:]], 0)
                sums[f, x, group * SPAN : (group + 1) * SPAN, :] = piece
            carried = turned[5 * SPAN :]
    second_half = place[1] == 1
    ny = grid.span_y
    for f in range(FIELDS):
        up[f] = sums[f, 4]
        down[f, :ny] = COUPLE * sums[f, 0, :ny] + gas[f, 0]
        down[f, ny:] = COUPLE * sums[f, 0, ny:]
        for x in range(5):
            low_row = COUPLE * sums[f, x, 0:1, :]
            if x < 4:
                low_row = low_row + gas[f, x, 0:1, :]
            high_row = COUPLE * sums[f, x, ny : ny + 1, :]
            row[x, f : f + 1, :] = jnp.where(second_half, low_row, high_row)
    for x in range(5):
        row[x, FIELDS:, :] = jnp.zeros((8 - FIELDS, grid.span_z), F32)


def sample_kernel(
    grid, last, bricks, place, stay, lower, upper, gas, sums, from_up, from_down,
    from_row, corner_low, corner_high, source, sampled, field, held
):
    ny = grid.span_y
    second_half = place[1] == 1
    at_end = place[0] == last
    face = jnp.where(second_half, 1.0, 0.0)
    for f in range(FIELDS):
        for x in range(5):
            extra = from_row[x, f : f + 1, :]
            if x == 0:
                extra = extra + corner_low[f : f + 1, :]
            if x == 4:
                extra = extra + corner_high[f : f + 1, :]
            first = row_numbers((8, grid.span_z)) == 0
            head = jnp.where(first, 2.0 * face * extra, 0.0)
            mine = sums[f, x, :ny, :]
            if x == 0:
                mine = mine + from_up[f, :ny, :]
            mine = jnp.concatenate([mine[:8] + head, mine[8:]], 0)
            tail = COUPLE * sums[f, x, ny : ny + 8, :]
            if x == 0:
                tail = tail + COUPLE * from_up[f, ny : ny + 8, :]
            if x < 4:
                source[f, x] = mine
                mine = gas[f, x] + COUPLE * mine
            else:
                mine = COUPLE * mine + from_down[f, :ny, :]
                mine = jnp.where(at_end, 0.0, mine)
                tail = tail + from_down[f, ny : ny + 8, :]
                tail = jnp.where(at_end, 0.0, tail)
                extra = jnp.where(at_end, 0.0, extra)
            tail = jnp.where(first & jnp.logical_not(second_half), tail + extra, 0.0)
            field[f, x, :ny, :] = mine
            field[f, x, ny : ny + 8, :] = tail
    for f in range(FIELDS):
        for group in range(grid.groups):
            edge = SPAN * (group + 1)
            pieces = [field[f, x, edge - SPAN : edge, :] for x in range(5)]
            if edge < grid.pad_y:
                pieces += [field[f, x, edge : edge + 1, :] for x in range(5)]
                pieces.append(jnp.zeros((3, grid.span_z), F32))
            else:
                pieces.append(jnp.zeros((8, grid.span_z), F32))
            turned = jnp.concatenate(pieces, 0).T
            at = (group * FIELDS + f) * grid.rows_z
            held[at : at + grid.span_z, :] = turned
            held[at + grid.span_z : at + grid.rows_z, :] = jnp.zeros((8, LANES), F32)

    offset = 0
    for part in (stay, lower, upper):
        blocks = part.shape[1] // LANES

        def step(turn, carry, part=part, offset=offset):
            for i in range(UNROLL):
                at = turn * UNROLL + i
                block = part[:, pl.ds(pl.multiple_of(at * LANES, LANES), LANES)]
                values = sample_block(grid, block, bricks[offset + at], held)
                lanes = pl.ds(pl.multiple_of((offset + at) * LANES, LANES), LANES)
                sampled[:, lanes] = values.astype(BF16)
            return carry

        lax.fori_loop(0, blocks // UNROLL, step, 0)
        offset += blocks


SMEM = pl.BlockSpec(memory_space=pltpu.SMEM)
VMEM = pl.BlockSpec(memory_space=pltpu.VMEM)


def shift(block, route):
    return lax.ppermute(block, ("axial", "radial"), route)


def per_device(load, offset, cell, rows, bricks, gas):
    axial = lax.axis_size("axial")
    radial = lax.axis_size("radial")
    span_y, span_z = gas.shape[2], gas.shape[3]
    grid = Grid(span_y, span_z)
    place = jnp.stack([lax.axis_index("axial"), lax.axis_index("radial")]).astype(jnp.int32)
    everyone = [(a, r) for a in range(axial) for r in range(radial)]

    def route(step_a, flip):
        return [
            (a * radial + r, (a + step_a) * radial + (radial - 1 - r if flip else r))
            for a, r in everyone
            if 0 <= a + step_a < axial
        ]

    up, down, stay = gather_call(load, offset, cell, rows)
    lower = shift(up, route(1, False))
    upper = shift(down, route(-1, False))
    big = pltpu.CompilerParams(vmem_limit_bytes=40 * 2**20)
    total = jax.ShapeDtypeStruct((grid.rows, LANES), F32)
    held = pl.pallas_call(
        functools.partial(deposit_stay_kernel, grid),
        out_shape=total,
        in_specs=[SMEM, VMEM],
        compiler_params=big,
        cost_estimate=pl.CostEstimate(flops=10**9, bytes_accessed=10**7, transcendentals=0),
        name="deposit_stay",
    )(bricks, stay)
    plane = jax.ShapeDtypeStruct((FIELDS, grid.pad_y, span_z), F32)
    sums, plane_up, plane_down, edge = pl.pallas_call(
        functools.partial(deposit_moved_kernel, grid),
        out_shape=(
            jax.ShapeDtypeStruct((FIELDS, 5, grid.pad_y, span_z), F32),
            plane,
            plane,
            jax.ShapeDtypeStruct((5, 8, span_z), F32),
        ),
        in_specs=[SMEM, SMEM, VMEM, VMEM, VMEM, VMEM],
        scratch_shapes=[pltpu.VMEM((grid.rows, LANES), F32)],
        compiler_params=big,
        name="deposit_moved",
    )(bricks, place, lower, upper, held, gas)
    from_up = shift(plane_up, route(1, False))
    from_down = shift(plane_down, route(-1, False))
    from_row = shift(edge, route(0, True))
    corner_low = shift(edge[4], route(1, True))
    corner_high = shift(edge[0], route(-1, True))
    return pl.pallas_call(
        functools.partial(sample_kernel, grid, axial - 1),
        out_shape=(
            jax.ShapeDtypeStruct(gas.shape, F32),
            jax.ShapeDtypeStruct((FIELDS, bricks.shape[0] * LANES), BF16),
        ),
        in_specs=[SMEM, SMEM] + [VMEM] * 10,
        scratch_shapes=[
            pltpu.VMEM((FIELDS, 5, grid.pad_y, span_z), F32),
            pltpu.VMEM((grid.rows, LANES), F32),
        ],
        compiler_params=big,
        name="sample",
    )(
        bricks, place, stay, lower, upper, gas, sums, from_up, from_down, from_row,
        corner_low, corner_high,
    )


def solution(mesh):
    return jax.shard_map(
        per_device,
        mesh=mesh,
        in_specs=(
            P(None, ("axial", "radial")),
            P(None, ("axial", "radial")),
            P(("axial", "radial")),
            P(None, ("axial", "radial")),
            P(("axial", "radial")),
            P(None, "axial", "radial", None),
        ),
        out_specs=(P(None, "axial", "radial", None), P(None, ("axial", "radial"))),
        check_vma=False,
    )
```

profile of v0, /device:TPU:32, one launch (start us, length us, event | category | flops | bytes accessed | tf_op | source)
XLA Modules:
  0.0 89.8 jit_solution(14534042037967638269)
XLA Ops:
  0.6 0.0 copy-start.1
  0.6 1.0 %copy-done.1 = f32[5,16384]{1,0:T(8,128)S(1)} copy-done((f32[5,16384]{1,0:T(8,128)S(1)}, f32[5,16384]{1,0:T(8,128)}, u32[]{:S(2)}) %copy-start.1) | copy-done | bytes 327704
  1.7 0.0 copy-start.2
  1.7 0.9 %copy-done.2 = f32[3,16384]{1,0:T(4,128)S(1)} copy-done((f32[3,16384]{1,0:T(4,128)S(1)}, f32[3,16384]{1,0:T(4,128)}, u32[]{:S(2)}) %copy-start.2) | copy-done | bytes 196632
  2.6 0.0 copy-start.3
  2.6 0.8 copy-done.3
  3.5 0.0 copy-start.4
  3.5 0.8 copy-done.4
  4.3 13.6 %gather_rows.1 = (f32[8,8192]{1,0:T(8,128)S(1)}, f32[8,8192]{1,0:T(8,128)S(1)}, f32[8,16384]{1,0:T(8,128)S(1)}) custom-call(f32[5,16384]{1,0:T(8,128)S(1)} %copy-done.1, f32[3,16384]{1,0:T(4,128)S(1)} %copy-done.2, s32[1,16384]{1,0:T(1,128)S(1)} %bitcast.7, s32[2,8192]{1,0:T(2,128)S(1)} %copy-done.4), custom_call_target="tpu_custom_call" | custom-call | tf_op jit(solution)/shard_map/gather_rows/pallas_call | solution.py:102
  17.9 1.9 %collective-permute-start = (f32[8,8192]{1,0:T(8,128)S(1)}, f32[8,8192]{1,0:T(8,128)S(1)}, u32[]{:S(2)}, u32[]{:S(2)}) collective-permute-start(f32[8,8192]{1,0:T(8,128)S(1)} %get-tuple-element.10), channel_id=1, source_target_pairs={{0,2},{1,3},{2,4},{3,5},{4,6},{5,7},{6,8},{7,9},{8,10},{9,11},{10,... | collective-permute-start | bytes 786440 | tf_op jit(solution)/shard_map/ppermute | solution.py:324
  19.8 5.8 %collective-permute-start.1 = (f32[8,8192]{1,0:T(8,128)S(1)}, f32[8,8192]{1,0:T(8,128)S(1)}, u32[]{:S(2)}, u32[]{:S(2)}) collective-permute-start(f32[8,8192]{1,0:T(8,128)S(1)} %get-tuple-element.11), channel_id=1, source_target_pairs={{2,0},{3,1},{4,2},{5,3},{6,4},{7,5},{8,6},{9,7},{10,8},{11,9},{12,... | collective-permute-start | bytes 786440 | tf_op jit(solution)/shard_map/ppermute | solution.py:324
  25.6 0.0 copy-start.5
  25.6 0.7 copy-done.5
  26.3 0.0 copy-start
  26.3 8.9 %deposit_stay.1.held = f32[3960,128]{1,0:T(8,128)S(1)} custom-call(s32[256]{0:T(256)S(1)} %copy-done.5, f32[8,16384]{1,0:T(8,128)S(1)} %get-tuple-element.9.parcels.stay), custom_call_target="tpu_custom_call" | custom-call | flops 1000000000 | bytes 10000000 | tf_op jit(solution)/shard_map/deposit_stay/pallas_call | solution.py:347
  35.2 0.1 pad_add_fusion.place
  35.3 0.0 copy-start.6
  35.3 0.0 collective-permute-done.lower
  35.3 0.0 collective-permute-done.1.upper
  35.3 0.0 copy-done
  35.3 9.8 %deposit_moved.1 = (f32[5,5,72,256]{3,2,1,0:T(8,128)S(1)}, f32[5,72,256]{2,1,0:T(8,128)S(1)}, f32[5,72,256]{2,1,0:T(8,128)S(1)}, f32[5,8,256]{2,1,0:T(8,128)S(1)}) custom-call(s32[256]{0:T(256)S(1)} %copy-done.5, s32[2]{0:T(128)S(1)} %pad_add_fusion.place, f32[8,8192]{1,0:T(8,128)S(1)} %collective-permute-done.lower, ...), custom_call_target="tpu_custom_call" | custom-call | tf_op jit(solution)/shard_map/deposit_moved/pallas_call | solution.py:356
  45.0 1.9 %collective-permute-start.2 = (f32[5,72,256]{2,1,0:T(8,128)S(1)}, f32[5,72,256]{2,1,0:T(8,128)S(1)}, u32[]{:S(2)}, u32[]{:S(2)}) collective-permute-start(f32[5,72,256]{2,1,0:T(8,128)S(1)} %get-tuple-element.13), channel_id=1, source_target_pairs={{0,2},{1,3},{2,4},{3,5},{4,6},{5,7},{6,8},{7,9},{8,10},{9,11},{10,... | collective-permute-start | bytes 1105928 | tf_op jit(solution)/shard_map/ppermute | solution.py:324
  47.0 5.8 %collective-permute-start.3 = (f32[5,72,256]{2,1,0:T(8,128)S(1)}, f32[5,72,256]{2,1,0:T(8,128)S(1)}, u32[]{:S(2)}, u32[]{:S(2)}) collective-permute-start(f32[5,72,256]{2,1,0:T(8,128)S(1)} %get-tuple-element.14), channel_id=1, source_target_pairs={{2,0},{3,1},{4,2},{5,3},{6,4},{7,5},{8,6},{9,7},{10,8},{11,9},{12,... | collective-permute-start | bytes 1105928 | tf_op jit(solution)/shard_map/ppermute | solution.py:324
  52.7 7.0 %collective-permute-start.4 = (f32[5,8,256]{2,1,0:T(8,128)S(1)}, f32[5,8,256]{2,1,0:T(8,128)S(1)}, u32[]{:S(2)}, u32[]{:S(2)}) collective-permute-start(f32[5,8,256]{2,1,0:T(8,128)S(1)} %get-tuple-element.15), channel_id=1, source_target_pairs={{0,1},{1,0},{2,3},{3,2},{4,5},{5,4},{6,7},{7,6},{8,9},{9,8},{10,11... | collective-permute-start | bytes 122888 | tf_op jit(solution)/shard_map/ppermute | solution.py:324
  59.8 1.9 %collective-permute-start.6 = (f32[8,256]{1,0:T(8,128)S(1)}, f32[8,256]{1,0:T(8,128)S(1)}, u32[]{:S(2)}, u32[]{:S(2)}) collective-permute-start(f32[8,256]{1,0:T(8,128)S(1)} %get-tuple-element.16), channel_id=1, source_target_pairs={{2,1},{3,0},{4,3},{5,2},{6,5},{7,4},{8,7},{9,6},{10,9},{11,8},{12,... | collective-permute-start | bytes 24584 | tf_op jit(solution)/shard_map/ppermute | solution.py:324
  61.7 7.5 %collective-permute-start.5 = (f32[8,256]{1,0:T(8,128)S(1)}, f32[8,256]{1,0:T(8,128)S(1)}, u32[]{:S(2)}, u32[]{:S(2)}) collective-permute-start(f32[8,256]{1,0:T(8,128)S(1)} %get-tuple-element.17), channel_id=1, source_target_pairs={{0,3},{1,2},{2,5},{3,4},{4,7},{5,6},{6,9},{7,8},{8,11},{9,10},{10,... | collective-permute-start | bytes 24584 | tf_op jit(solution)/shard_map/ppermute | solution.py:324
  69.3 0.0 collective-permute-done.6.corner_high
  69.3 2.5 %collective-permute-done.5.corner_low = f32[8,256]{1,0:T(8,128)S(1)} collective-permute-done((f32[8,256]{1,0:T(8,128)S(1)}, f32[8,256]{1,0:T(8,128)S(1)}, u32[]{:S(2)}, u32[]{:S(2)}) %collective-permute-start.5) | collective-permute-done | bytes 8224 | tf_op jit(solution)/shard_map/ppermute | solution.py:324
  71.8 0.0 collective-permute-done.4.from_row
  71.8 0.0 collective-permute-done.2.from_up
  71.8 0.0 collective-permute-done.3.from_down
  71.8 0.0 copy-done.6
  71.8 18.0 %sample.1 = (f32[5,4,64,256]{3,2,1,0:T(8,128)}, bf16[5,32768]{1,0:T(8,128)(2,1)}) custom-call(s32[256]{0:T(256)S(1)} %copy-done.6, s32[2]{0:T(128)S(1)} %pad_add_fusion.place, f32[8,16384]{1,0:T(8,128)S(1)} %get-tuple-element.9.parcels.stay, f32[8,8192]{1,0:T(8,128)S(1)} %collective-permute-done.lower, f32[8,8192]{1,0:T(8,128)S(1)} %collective-permute-done.1.upper, ...), custom_call_target="tpu_custom_call" | custom-call | tf_op jit(solution)/shard_map/sample/pallas_call | solution.py:374
  (1 shorter events, 0.0 us)
Async XLA Ops:
  0.6 1.0 %copy-start.1 = (f32[5,16384]{1,0:T(8,128)S(1)}, f32[5,16384]{1,0:T(8,128)}, u32[]{:S(2)}) copy-start(f32[5,16384]{1,0:T(8,128)} %load.1) | copy-start | bytes 983044
  1.7 0.9 %copy-start.2 = (f32[3,16384]{1,0:T(4,128)S(1)}, f32[3,16384]{1,0:T(4,128)}, u32[]{:S(2)}) copy-start(f32[3,16384]{1,0:T(4,128)} %offset.1) | copy-start | bytes 589828
  2.6 0.8 copy-start.3
  3.5 0.8 copy-start.4
  17.9 17.4 %collective-permute-start = (f32[8,8192]{1,0:T(8,128)S(1)}, f32[8,8192]{1,0:T(8,128)S(1)}, u32[]{:S(2)}, u32[]{:S(2)}) collective-permute-start(f32[8,8192]{1,0:T(8,128)S(1)} %get-tuple-element.10), channel_id=1, source_target_pairs={{0,2},{1,3},{2,4},{3,5},{4,6},{5,7},{6,8},{7,9},{8,10},{9,11},{10,... | collective-permute-start | bytes 786440 | tf_op jit(solution)/shard_map/ppermute | solution.py:324
  19.8 15.4 %collective-permute-start.1 = (f32[8,8192]{1,0:T(8,128)S(1)}, f32[8,8192]{1,0:T(8,128)S(1)}, u32[]{:S(2)}, u32[]{:S(2)}) collective-permute-start(f32[8,8192]{1,0:T(8,128)S(1)} %get-tuple-element.11), channel_id=1, source_target_pairs={{2,0},{3,1},{4,2},{5,3},{6,4},{7,5},{8,6},{9,7},{10,8},{11,9},{12,... | collective-permute-start | bytes 786440 | tf_op jit(solution)/shard_map/ppermute | solution.py:324
  25.6 0.7 copy-start.5
  26.3 9.0 %copy-start = (f32[5,4,64,256]{3,2,1,0:T(8,128)S(1)}, f32[5,4,64,256]{3,2,1,0:T(8,128)}, u32[]{:S(2)}) copy-start(f32[5,4,64,256]{3,2,1,0:T(8,128)} %gas.3) | copy-start | bytes 3932164
  35.3 36.5 %copy-start.6 = (s32[256]{0:T(256)S(1)}, s32[256]{0:T(256)}, u32[]{:S(2)}) copy-start(s32[256]{0:T(256)} %bricks.5) | copy-start | bytes 3076
  45.0 26.8 %collective-permute-start.2 = (f32[5,72,256]{2,1,0:T(8,128)S(1)}, f32[5,72,256]{2,1,0:T(8,128)S(1)}, u32[]{:S(2)}, u32[]{:S(2)}) collective-permute-start(f32[5,72,256]{2,1,0:T(8,128)S(1)} %get-tuple-element.13), channel_id=1, source_target_pairs={{0,2},{1,3},{2,4},{3,5},{4,6},{5,7},{6,8},{7,9},{8,10},{9,11},{10,... | collective-permute-start | bytes 1105928 | tf_op jit(solution)/shard_map/ppermute | solution.py:324
  47.0 24.8 %collective-permute-start.3 = (f32[5,72,256]{2,1,0:T(8,128)S(1)}, f32[5,72,256]{2,1,0:T(8,128)S(1)}, u32[]{:S(2)}, u32[]{:S(2)}) collective-permute-start(f32[5,72,256]{2,1,0:T(8,128)S(1)} %get-tuple-element.14), channel_id=1, source_target_pairs={{2,0},{3,1},{4,2},{5,3},{6,4},{7,5},{8,6},{9,7},{10,8},{11,9},{12,... | collective-permute-start | bytes 1105928 | tf_op jit(solution)/shard_map/ppermute | solution.py:324
  52.7 19.1 %collective-permute-start.4 = (f32[5,8,256]{2,1,0:T(8,128)S(1)}, f32[5,8,256]{2,1,0:T(8,128)S(1)}, u32[]{:S(2)}, u32[]{:S(2)}) collective-permute-start(f32[5,8,256]{2,1,0:T(8,128)S(1)} %get-tuple-element.15), channel_id=1, source_target_pairs={{0,1},{1,0},{2,3},{3,2},{4,5},{5,4},{6,7},{7,6},{8,9},{9,8},{10,11... | collective-permute-start | bytes 122888 | tf_op jit(solution)/shard_map/ppermute | solution.py:324
  59.8 9.5 %collective-permute-start.6 = (f32[8,256]{1,0:T(8,128)S(1)}, f32[8,256]{1,0:T(8,128)S(1)}, u32[]{:S(2)}, u32[]{:S(2)}) collective-permute-start(f32[8,256]{1,0:T(8,128)S(1)} %get-tuple-element.16), channel_id=1, source_target_pairs={{2,1},{3,0},{4,3},{5,2},{6,5},{7,4},{8,7},{9,6},{10,9},{11,8},{12,... | collective-permute-start | bytes 24584 | tf_op jit(solution)/shard_map/ppermute | solution.py:324
  61.7 10.1 %collective-permute-start.5 = (f32[8,256]{1,0:T(8,128)S(1)}, f32[8,256]{1,0:T(8,128)S(1)}, u32[]{:S(2)}, u32[]{:S(2)}) collective-permute-start(f32[8,256]{1,0:T(8,128)S(1)} %get-tuple-element.17), channel_id=1, source_target_pairs={{0,3},{1,2},{2,5},{3,4},{4,7},{5,6},{6,9},{7,8},{8,11},{9,10},{10,... | collective-permute-start | bytes 24584 | tf_op jit(solution)/shard_map/ppermute | solution.py:324
where the time goes:
time: 90.2 us; the launch traced here: 89.8 us
  Pallas kernels  50.3 us (56%)
  starting transfers between devices  31.9 us (35%)
  local copies, waits for them, and re-layouts  4.35 us (5%)
  waiting for transfers between devices  2.54 us (3%)
    ppermute x7, starting transfers between devices, shift(): return lax.ppermute(block, ('axial', 'radial'), route)  31.9 us
    pallas_call x1, Pallas kernels, per_device(): pl.pallas_call(functools.partial(sample_kernel, grid, axial - 1), out_sha...  18 us
    pallas_call x1, Pallas kernels, gather_call(): pl.pallas_call(gather_kernel, out_shape=(moved, moved, jax.ShapeDtypeStru...  13.6 us
    pallas_call x1, Pallas kernels, per_device(): pl.pallas_call(functools.partial(deposit_moved_kernel, grid), out_shape=(...  9.76 us
    pallas_call x1, Pallas kernels, per_device(): pl.pallas_call(functools.partial(deposit_stay_kernel, grid), out_shape=to...  8.9 us
    unnamed x14, local copies, waits for them, and re-layouts  4.34 us
    ppermute x7, waiting for transfers between devices, shift(): return lax.ppermute(block, ('axial', 'radial'), route)  2.54 us
  transfers between devices with their start and end apart: 7, of which 1 were waited for; matrix products, arithmetic and copies ran while one was open for 0% of the time, Pallas kernels for 10%

commit v1 on v0

--- a/solution.py
+++ b/solution.py
@@ -9,7 +9,8 @@
 
 COUPLE = 0.5
 LANES = 128
-TILE = 256
+TILE = 2048
+CHUNK = 32
 FIELDS = 5
 GROUP = 6
 SPAN = 4 * GROUP
@@ -70,14 +71,14 @@
             wanted = jnp.concatenate([lane_hot, lane_hot], 0)
             block8 = jnp.broadcast_to(block, (8, TILE))
             found = jnp.zeros((8, TILE), F32)
-            for chunk in range(blocks // 16):
+            for chunk in range(blocks // CHUNK):
                 part = jnp.dot(
-                    table[chunk * 128 : chunk * 128 + 128, :], wanted,
+                    table[8 * CHUNK * chunk : 8 * CHUNK * (chunk + 1), :], wanted,
                     preferred_element_type=F32,
                 )
-                for i in range(16):
+                for i in range(CHUNK):
                     found = jnp.where(
-                        block8 == chunk * 16 + i, part[8 * i : 8 * i + 8, :], found
+                        block8 == chunk * CHUNK + i, part[8 * i : 8 * i + 8, :], found
                     )
             out[:, pl.ds(at, TILE)] = found
             return carry
@@ -184,7 +185,7 @@
     )
 
 
-UNROLL = 4
+UNROLL = 32
 
 
 def deposit_loop(grid, parcels, bricks, offset, count, total):
@@ -324,6 +325,162 @@
     return lax.ppermute(block, ("axial", "radial"), route)
 
 
+BIG = pltpu.CompilerParams(vmem_limit_bytes=24 * 2**20)
+
+
+def deposit_stay_call(grid, bricks, stay):
+    return pl.pallas_call(
+        functools.partial(deposit_stay_kernel, grid),
+        out_shape=jax.ShapeDtypeStruct((grid.rows, LANES), F32),
+        in_specs=[SMEM, VMEM],
+        compiler_params=BIG,
+        cost_estimate=pl.CostEstimate(flops=10**9, bytes_accessed=10**7, transcendentals=0),
+        name="deposit_stay",
+    )(bricks, stay)
+
+
+def deposit_moved_call(grid, bricks, place, lower, upper, held, gas):
+    plane = jax.ShapeDtypeStruct((FIELDS, grid.pad_y, grid.span_z), F32)
+    return pl.pallas_call(
+        functools.partial(deposit_moved_kernel, grid),
+        out_shape=(
+            jax.ShapeDtypeStruct((FIELDS, 5, grid.pad_y, grid.span_z), F32),
+            plane,
+            plane,
+            jax.ShapeDtypeStruct((5, 8, grid.span_z), F32),
+        ),
+        in_specs=[SMEM, SMEM, VMEM, VMEM, VMEM, VMEM],
+        scratch_shapes=[pltpu.VMEM((grid.rows, LANES), F32)],
+        compiler_params=BIG,
+        name="deposit_moved",
+    )(bricks, place, lower, upper, held, gas)
+
+
+def exchange_kernel(
+    last, up, down, edge, from_up, from_down, from_row, corner_low, corner_high, sent, got
+):
+    a = lax.axis_index("axial")
+    r = lax.axis_index("radial")
+    has_above = a < last
+    has_below = a > 0
+    barrier = pltpu.get_barrier_semaphore()
+
+    def greet(axial_at, radial_at):
+        pl.semaphore_signal(
+            barrier, inc=1, device_id=(axial_at, radial_at),
+            device_id_type=pl.DeviceIdType.MESH,
+        )
+
+    greet(a, 1 - r)
+
+    @pl.when(has_above)
+    def _():
+        greet(a + 1, r)
+        greet(a + 1, 1 - r)
+
+    @pl.when(has_below)
+    def _():
+        greet(a - 1, r)
+        greet(a - 1, 1 - r)
+
+    peers = 1 + 2 * has_above.astype(jnp.int32) + 2 * has_below.astype(jnp.int32)
+    pl.semaphore_wait(barrier, peers)
+
+    def copy(number, source, target, axial_at, radial_at):
+        return pltpu.make_async_remote_copy(
+            src_ref=source, dst_ref=target, send_sem=sent.at[number],
+            recv_sem=got.at[number], device_id=(axial_at, radial_at),
+            device_id_type=pl.DeviceIdType.MESH,
+        )
+
+    row = copy(0, edge, from_row, a, 1 - r)
+    above = (
+        copy(1, up, from_up, a + 1, r),
+        copy(2, edge.at[4], corner_low, a + 1, 1 - r),
+    )
+    below = (
+        copy(3, down, from_down, a - 1, r),
+        copy(4, edge.at[0], corner_high, a - 1, 1 - r),
+    )
+
+    @pl.when(has_above)
+    def _():
+        for each in above:
+            each.start()
+
+    @pl.when(has_below)
+    def _():
+        for each in below:
+            each.start()
+
+    row.start()
+
+    @pl.when(jnp.logical_not(has_below))
+    def _():
+        from_up[...] = jnp.zeros_like(from_up)
+        corner_low[...] = jnp.zeros_like(corner_low)
+
+    @pl.when(jnp.logical_not(has_above))
+    def _():
+        from_down[...] = jnp.zeros_like(from_down)
+        corner_high[...] = jnp.zeros_like(corner_high)
+
+    row.wait()
+
+    @pl.when(has_above)
+    def _():
+        for each in above:
+            each.wait_send()
+        for each in below:
+            each.wait_recv()
+
+    @pl.when(has_below)
+    def _():
+        for each in below:
+            each.wait_send()
+        for each in above:
+            each.wait_recv()
+
+
+def exchange_call(last, up, down, edge):
+    corner = jax.ShapeDtypeStruct(edge.shape[1:], F32)
+    return pl.pallas_call(
+        functools.partial(exchange_kernel, last),
+        out_shape=(
+            jax.ShapeDtypeStruct(up.shape, F32),
+            jax.ShapeDtypeStruct(down.shape, F32),
+            jax.ShapeDtypeStruct(edge.shape, F32),
+            corner,
+            corner,
+        ),
+        in_specs=[VMEM] * 3,
+        out_specs=(VMEM,) * 5,
+        scratch_shapes=[pltpu.SemaphoreType.DMA((5,)), pltpu.SemaphoreType.DMA((5,))],
+        compiler_params=pltpu.CompilerParams(
+            collective_id=0, has_side_effects=True, vmem_limit_bytes=4 * 2**20
+        ),
+        name="exchange",
+    )(up, down, edge)
+
+
+def sample_call(grid, last, bricks, place, *arrays):
+    gas = arrays[3]
+    return pl.pallas_call(
+        functools.partial(sample_kernel, grid, last),
+        out_shape=(
+            jax.ShapeDtypeStruct(gas.shape, F32),
+            jax.ShapeDtypeStruct((FIELDS, bricks.shape[0] * LANES), BF16),
+        ),
+        in_specs=[SMEM, SMEM] + [VMEM] * 10,
+        scratch_shapes=[
+            pltpu.VMEM((FIELDS, 5, grid.pad_y, grid.span_z), F32),
+            pltpu.VMEM((grid.rows, LANES), F32),
+        ],
+        compiler_params=BIG,
+        name="sample",
+    )(bricks, place, *arrays)
+
+
 def per_device(load, offset, cell, rows, bricks, gas):
     axial = lax.axis_size("axial")
     radial = lax.axis_size("radial")
@@ -342,51 +499,13 @@
     up, down, stay = gather_call(load, offset, cell, rows)
     lower = shift(up, route(1, False))
     upper = shift(down, route(-1, False))
-    big = pltpu.CompilerParams(vmem_limit_bytes=40 * 2**20)
-    total = jax.ShapeDtypeStruct((grid.rows, LANES), F32)
-    held = pl.pallas_call(
-        functools.partial(deposit_stay_kernel, grid),
-        out_shape=total,
-        in_specs=[SMEM, VMEM],
-        compiler_params=big,
-        cost_estimate=pl.CostEstimate(flops=10**9, bytes_accessed=10**7, transcendentals=0),
-        name="deposit_stay",
-    )(bricks, stay)
-    plane = jax.ShapeDtypeStruct((FIELDS, grid.pad_y, span_z), F32)
-    sums, plane_up, plane_down, edge = pl.pallas_call(
-        functools.partial(deposit_moved_kernel, grid),
-        out_shape=(
-            jax.ShapeDtypeStruct((FIELDS, 5, grid.pad_y, span_z), F32),
-            plane,
-            plane,
-            jax.ShapeDtypeStruct((5, 8, span_z), F32),
-        ),
-        in_specs=[SMEM, SMEM, VMEM, VMEM, VMEM, VMEM],
-        scratch_shapes=[pltpu.VMEM((grid.rows, LANES), F32)],
-        compiler_params=big,
-        name="deposit_moved",
-    )(bricks, place, lower, upper, held, gas)
-    from_up = shift(plane_up, route(1, False))
-    from_down = shift(plane_down, route(-1, False))
-    from_row = shift(edge, route(0, True))
-    corner_low = shift(edge[4], route(1, True))
-    corner_high = shift(edge[0], route(-1, True))
-    return pl.pallas_call(
-        functools.partial(sample_kernel, grid, axial - 1),
-        out_shape=(
-            jax.ShapeDtypeStruct(gas.shape, F32),
-            jax.ShapeDtypeStruct((FIELDS, bricks.shape[0] * LANES), BF16),
-        ),
-        in_specs=[SMEM, SMEM] + [VMEM] * 10,
-        scratch_shapes=[
-            pltpu.VMEM((FIELDS, 5, grid.pad_y, span_z), F32),
-            pltpu.VMEM((grid.rows, LANES), F32),
-        ],
-        compiler_params=big,
-        name="sample",
-    )(
-        bricks, place, stay, lower, upper, gas, sums, from_up, from_down, from_row,
-        corner_low, corner_high,
+    held = deposit_stay_call(grid, bricks, stay)
+    sums, plane_up, plane_down, edge = deposit_moved_call(
+        grid, bricks, place, lower, upper, held, gas
+    )
+    arrived = exchange_call(axial - 1, plane_up, plane_down, edge)
+    return sample_call(
+        grid, axial - 1, bricks, place, stay, lower, upper, gas, sums, *arrived
     )
 
 

time: 90.2 us -> 57.1 us (0.63)
  the two profiles are of different devices: /device:TPU:32 before, /device:TPU:2 now
where the time goes in v1:
time: 57.1 us; the launch traced here: 56.8 us
  Pallas kernels  41.3 us (72%)
  starting transfers between devices  10.4 us (18%)
  local copies, waits for them, and re-layouts  4.34 us (8%)
  between operations  0.72 us (1%)
    pallas_call x1, Pallas kernels, exchange_call(): pl.pallas_call(functools.partial(exchange_kernel, last), out_shape=(jax.S...  19.4 us
    ppermute x2, starting transfers between devices, shift(): return lax.ppermute(block, ('axial', 'radial'), route)  10.4 us
    pallas_call x1, Pallas kernels, sample_call(): pl.pallas_call(functools.partial(sample_kernel, grid, last), out_shape=(j...  9.36 us
    pallas_call x1, Pallas kernels, deposit_moved_call(): pl.pallas_call(functools.partial(deposit_moved_kernel, grid), out_shape=(...  4.75 us
    unnamed x14, local copies, waits for them, and re-layouts  4.34 us
    pallas_call x1, Pallas kernels, gather_call(): pl.pallas_call(gather_kernel, out_shape=(moved, moved, jax.ShapeDtypeStru...  3.91 us
    pallas_call x1, Pallas kernels, deposit_stay_call(): pl.pallas_call(functools.partial(deposit_stay_kernel, grid), out_shape=ja...  3.85 us
  transfers between devices with their start and end apart: 2, of which 0 were waited for; matrix products, arithmetic and copies ran while one was open for 0% of the time, Pallas kernels for 7%

profile of v1, /device:TPU:2, one launch (start us, length us, event | category | flops | bytes accessed | tf_op | source)
XLA Modules:
  0.0 56.8 jit_solution(12056330535654325283)
XLA Ops:
  0.6 0.0 copy-start.1
  0.6 1.0 %copy-done.1 = f32[5,16384]{1,0:T(8,128)S(1)} copy-done((f32[5,16384]{1,0:T(8,128)S(1)}, f32[5,16384]{1,0:T(8,128)}, u32[]{:S(2)}) %copy-start.1) | copy-done | bytes 327704
  1.7 0.0 copy-start.2
  1.7 0.9 %copy-done.2 = f32[3,16384]{1,0:T(4,128)S(1)} copy-done((f32[3,16384]{1,0:T(4,128)S(1)}, f32[3,16384]{1,0:T(4,128)}, u32[]{:S(2)}) %copy-start.2) | copy-done | bytes 196632
  2.6 0.0 copy-start.3
  2.6 0.8 %copy-done.3 = s32[16384]{0:T(1024)S(1)} copy-done((s32[16384]{0:T(1024)S(1)}, s32[16384]{0:T(1024)}, u32[]{:S(2)}) %copy-start.3) | copy-done | bytes 65560
  3.5 0.0 copy-start.4
  3.5 0.8 %copy-done.4 = s32[2,8192]{1,0:T(2,128)S(1)} copy-done((s32[2,8192]{1,0:T(2,128)S(1)}, s32[2,8192]{1,0:T(2,128)}, u32[]{:S(2)}) %copy-start.4) | copy-done | bytes 65560
  4.3 3.9 %gather_rows.1 = (f32[8,8192]{1,0:T(8,128)S(1)}, f32[8,8192]{1,0:T(8,128)S(1)}, f32[8,16384]{1,0:T(8,128)S(1)}) custom-call(f32[5,16384]{1,0:T(8,128)S(1)} %copy-done.1, f32[3,16384]{1,0:T(4,128)S(1)} %copy-done.2, s32[1,16384]{1,0:T(1,128)S(1)} %bitcast.3, s32[2,8192]{1,0:T(2,128)S(1)} %copy-done.4), custom_call_target="tpu_custom_call" | custom-call | tf_op jit(solution)/shard_map/gather_rows/pallas_call | solution.py:103
  8.2 1.9 %collective-permute-start = (f32[8,8192]{1,0:T(8,128)S(1)}, f32[8,8192]{1,0:T(8,128)S(1)}, u32[]{:S(2)}, u32[]{:S(2)}) collective-permute-start(f32[8,8192]{1,0:T(8,128)S(1)} %get-tuple-element.15), channel_id=1, source_target_pairs={{0,2},{1,3},{2,4},{3,5},{4,6},{5,7},{6,8},{7,9},{8,10},{9,11},{10,... | collective-permute-start | bytes 786440 | tf_op jit(solution)/shard_map/ppermute | solution.py:325
  10.2 8.4 %collective-permute-start.1 = (f32[8,8192]{1,0:T(8,128)S(1)}, f32[8,8192]{1,0:T(8,128)S(1)}, u32[]{:S(2)}, u32[]{:S(2)}) collective-permute-start(f32[8,8192]{1,0:T(8,128)S(1)} %get-tuple-element.16), channel_id=1, source_target_pairs={{2,0},{3,1},{4,2},{5,3},{6,4},{7,5},{8,6},{9,7},{10,8},{11,9},{12,... | collective-permute-start | bytes 786440 | tf_op jit(solution)/shard_map/ppermute | solution.py:325
  18.6 0.0 copy-start.5
  18.6 0.7 %copy-done.5 = s32[256]{0:T(256)S(1)} copy-done((s32[256]{0:T(256)S(1)}, s32[256]{0:T(256)}, u32[]{:S(2)}) %copy-start.5) | copy-done | bytes 1048
  19.3 0.0 copy-start
  19.3 3.9 %deposit_stay.1.held = f32[3960,128]{1,0:T(8,128)S(1)} custom-call(s32[256]{0:T(256)S(1)} %copy-done.5, f32[8,16384]{1,0:T(8,128)S(1)} %get-tuple-element.14.parcels.stay), custom_call_target="tpu_custom_call" | custom-call | flops 1000000000 | bytes 10000000 | tf_op jit(solution)/shard_map/deposit_stay/pallas_call | solution.py:332
  23.2 0.1 pad_add_fusion.place
  23.2 0.0 copy-start.6
  23.2 0.0 collective-permute-done.lower
  23.2 0.0 collective-permute-done.1.upper
  23.2 0.0 copy-done
  23.3 4.8 %deposit_moved.1 = (f32[5,5,72,256]{3,2,1,0:T(8,128)S(1)}, f32[5,72,256]{2,1,0:T(8,128)S(1)}, f32[5,72,256]{2,1,0:T(8,128)S(1)}, f32[5,8,256]{2,1,0:T(8,128)S(1)}) custom-call(s32[256]{0:T(256)S(1)} %copy-done.5, s32[2]{0:T(128)S(1)} %pad_add_fusion.place, f32[8,8192]{1,0:T(8,128)S(1)} %collective-permute-done.lower, ...), custom_call_target="tpu_custom_call" | custom-call | tf_op jit(solution)/shard_map/deposit_moved/pallas_call | solution.py:344
  28.0 19.4 %exchange.1 = (f32[5,72,256]{2,1,0:T(8,128)S(1)}, f32[5,72,256]{2,1,0:T(8,128)S(1)}, f32[5,8,256]{2,1,0:T(8,128)S(1)}, f32[8,256]{1,0:T(8,128)S(1)}, f32[8,256]{1,0:T(8,128)S(1)}) custom-call(f32[5,72,256]{2,1,0:T(8,128)S(1)} %get-tuple-element.18.up, f32[5,72,256]{2,1,0:T(8,128)S(1)} %get-tuple-element.19.down, f32[5,8,256]{2,1,0:T(8,128)S(1)} %get-tuple-element.20.edge), custom_call_target="tpu_custom_call" | custom-call | tf_op jit(solution)/shard_map/exchange/pallas_call | solution.py:447
  47.4 0.0 copy-done.6
  47.4 9.4 %sample.1 = (f32[5,4,64,256]{3,2,1,0:T(8,128)}, bf16[5,32768]{1,0:T(8,128)(2,1)}) custom-call(s32[256]{0:T(256)S(1)} %copy-done.6, s32[2]{0:T(128)S(1)} %pad_add_fusion.place, f32[8,16384]{1,0:T(8,128)S(1)} %get-tuple-element.14.parcels.stay, f32[8,8192]{1,0:T(8,128)S(1)} %collective-permute-done.lower, f32[8,8192]{1,0:T(8,128)S(1)} %collective-permute-done.1.upper, ...), custom_call_target="tpu_custom_call" | custom-call | tf_op jit(solution)/shard_map/sample/pallas_call | solution.py:468
Async XLA Ops:
  0.6 1.0 %copy-start.1 = (f32[5,16384]{1,0:T(8,128)S(1)}, f32[5,16384]{1,0:T(8,128)}, u32[]{:S(2)}) copy-start(f32[5,16384]{1,0:T(8,128)} %load.1) | copy-start | bytes 983044
  1.7 0.9 %copy-start.2 = (f32[3,16384]{1,0:T(4,128)S(1)}, f32[3,16384]{1,0:T(4,128)}, u32[]{:S(2)}) copy-start(f32[3,16384]{1,0:T(4,128)} %offset.1) | copy-start | bytes 589828
  2.6 0.8 %copy-start.3 = (s32[16384]{0:T(1024)S(1)}, s32[16384]{0:T(1024)}, u32[]{:S(2)}) copy-start(s32[16384]{0:T(1024)} %param.8) | copy-start | bytes 196612
  3.5 0.8 %copy-start.4 = (s32[2,8192]{1,0:T(2,128)S(1)}, s32[2,8192]{1,0:T(2,128)}, u32[]{:S(2)}) copy-start(s32[2,8192]{1,0:T(2,128)} %rows.1) | copy-start | bytes 196612
  8.2 15.0 %collective-permute-start = (f32[8,8192]{1,0:T(8,128)S(1)}, f32[8,8192]{1,0:T(8,128)S(1)}, u32[]{:S(2)}, u32[]{:S(2)}) collective-permute-start(f32[8,8192]{1,0:T(8,128)S(1)} %get-tuple-element.15), channel_id=1, source_target_pairs={{0,2},{1,3},{2,4},{3,5},{4,6},{5,7},{6,8},{7,9},{8,10},{9,11},{10,... | collective-permute-start | bytes 786440 | tf_op jit(solution)/shard_map/ppermute | solution.py:325
  10.2 13.1 %collective-permute-start.1 = (f32[8,8192]{1,0:T(8,128)S(1)}, f32[8,8192]{1,0:T(8,128)S(1)}, u32[]{:S(2)}, u32[]{:S(2)}) collective-permute-start(f32[8,8192]{1,0:T(8,128)S(1)} %get-tuple-element.16), channel_id=1, source_target_pairs={{2,0},{3,1},{4,2},{5,3},{6,4},{7,5},{8,6},{9,7},{10,8},{11,9},{12,... | collective-permute-start | bytes 786440 | tf_op jit(solution)/shard_map/ppermute | solution.py:325
  18.6 0.7 %copy-start.5 = (s32[256]{0:T(256)S(1)}, s32[256]{0:T(256)}, u32[]{:S(2)}) copy-start(s32[256]{0:T(256)} %bricks.5) | copy-start | bytes 3076
  19.3 4.0 %copy-start = (f32[5,4,64,256]{3,2,1,0:T(8,128)S(1)}, f32[5,4,64,256]{3,2,1,0:T(8,128)}, u32[]{:S(2)}) copy-start(f32[5,4,64,256]{3,2,1,0:T(8,128)} %gas.3) | copy-start | bytes 3932164
  23.2 24.2 %copy-start.6 = (s32[256]{0:T(256)S(1)}, s32[256]{0:T(256)}, u32[]{:S(2)}) copy-start(s32[256]{0:T(256)} %bricks.5) | copy-start | bytes 3076

commit v2 on v1

--- a/solution.py
+++ b/solution.py
@@ -32,7 +32,22 @@
     return lax.broadcasted_iota(jnp.int32, shape, 0)
 
 
-def gather_kernel(load, offset, cell, rows, up, down, stay, table, base, corner, gone):
+def gather_kernel(
+    load_in, offset_in, cell_in, rows_in, bricks_in, up, down, stay, bricks, load, offset,
+    cell, rows, table, base, corner, gone, arrived
+):
+    pairs = (
+        (cell_in, cell), (load_in, load), (offset_in, offset), (rows_in, rows),
+        (bricks_in, bricks),
+    )
+    copies = [
+        pltpu.make_async_copy(source, target, arrived.at[i])
+        for i, (source, target) in enumerate(pairs)
+    ]
+    for each in copies:
+        each.start()
+    for each in copies:
+        each.wait()
     count = load.shape[1]
     blocks = count // LANES
     slots = rows.shape[1]
@@ -96,22 +111,33 @@
     lax.fori_loop(0, blocks, keep, 0, unroll=8)
 
 
-def gather_call(load, offset, cell, rows):
+def gather_call(load, offset, cell, rows, bricks):
     count = load.shape[1]
     slots = rows.shape[1]
     moved = jax.ShapeDtypeStruct((8, slots), F32)
     return pl.pallas_call(
         gather_kernel,
-        out_shape=(moved, moved, jax.ShapeDtypeStruct((8, count), F32)),
+        out_shape=(
+            moved,
+            moved,
+            jax.ShapeDtypeStruct((8, count), F32),
+            jax.ShapeDtypeStruct(bricks.shape, jnp.int32),
+        ),
+        in_specs=[pl.BlockSpec(memory_space=pltpu.HBM)] * 5,
         scratch_shapes=[
+            pltpu.VMEM(load.shape, F32),
+            pltpu.VMEM(offset.shape, F32),
+            pltpu.VMEM((1, count), jnp.int32),
+            pltpu.VMEM(rows.shape, jnp.int32),
             pltpu.VMEM((8 * (count // LANES), 2 * LANES), BF16),
             pltpu.VMEM((8, count), F32),
             pltpu.VMEM((8, count), F32),
             pltpu.VMEM((count // LANES, LANES), F32),
+            pltpu.SemaphoreType.DMA((5,)),
         ],
-        compiler_params=pltpu.CompilerParams(vmem_limit_bytes=24 * 2**20),
+        compiler_params=pltpu.CompilerParams(vmem_limit_bytes=16 * 2**20),
         name="gather_rows",
-    )(load, offset, cell.reshape(1, count), rows)
+    )(load, offset, cell.reshape(1, count), rows, bricks)
 
 
 class Grid:
@@ -166,10 +192,8 @@
         total[rows, :] += summed[8 * f : 8 * f + 8]
 
 
-def sample_block(grid, block, brick, held):
-    first, shift_y = grid.place(brick)
-    high, low = plane_weights(block, shift_y)
-    plane = jnp.concatenate([high.astype(BF16), low.astype(BF16)], 0)
+def sample_block(grid, block, brick, plane, held):
+    first, _ = grid.place(brick)
     fields = jnp.concatenate(
         [held[pl.ds(first + f * grid.rows_z, 8), :] for f in range(FIELDS)], 0
     )
@@ -204,14 +228,15 @@
     deposit_loop(grid, parcels, bricks, 0, parcels.shape[1] // LANES, total)
 
 
-def deposit_moved_kernel(
-    grid, bricks, place, lower, upper, held, gas, sums, up, down, row, total
-):
+def deposit_moved_kernel(grid, bricks, lower, upper, held, total):
     total[...] = held[...]
     blocks = lower.shape[1] // LANES
     start = bricks.shape[0] - 2 * blocks
     deposit_loop(grid, lower, bricks, start, blocks, total)
     deposit_loop(grid, upper, bricks, start + blocks, blocks, total)
+
+
+def merge_selector():
     picked = row_numbers((160, LANES))
     lane = lax.broadcasted_iota(jnp.int32, (160, LANES), 1)
     edge = picked - 5 * SPAN
@@ -219,40 +244,41 @@
         picked < 5 * SPAN, picked, jnp.where(edge % 8 == 0, 5 * SPAN + edge // 8, -1)
     )
     select = jnp.where(lane == wanted, 1.0, 0.0).astype(BF16)
-    select = jnp.concatenate([select, select], 1)
-    for f in range(FIELDS):
-        carried = None
-        for group in range(grid.groups):
-            first = (group * FIELDS + f) * grid.rows_z
-            high, low = split(total[first : first + grid.span_z, :])
-            both = jnp.concatenate([high.astype(BF16), low.astype(BF16)], 1)
-            turned = lax.dot_general(select, both, NT, preferred_element_type=F32)
-            for x in range(5):
-                piece = turned[x * SPAN : (x + 1) * SPAN]
-                if carried is not None:
-                    head = piece[:8] + carried[8 * x : 8 * x + 8]
-                    piece = jnp.concatenate([head, piece[8:]], 0)
-                sums[f, x, group * SPAN : (group + 1) * SPAN, :] = piece
-            carried = turned[5 * SPAN :]
-    second_half = place[1] == 1
+    return jnp.concatenate([select, select], 1)
+
+
+def merge_field(grid, f, select, total, sums):
+    carried = None
+    for group in range(grid.groups):
+        first = (group * FIELDS + f) * grid.rows_z
+        high, low = split(total[first : first + grid.span_z, :])
+        both = jnp.concatenate([high.astype(BF16), low.astype(BF16)], 1)
+        turned = lax.dot_general(select, both, NT, preferred_element_type=F32)
+        for x in range(5):
+            piece = turned[x * SPAN : (x + 1) * SPAN]
+            if carried is not None:
+                head = piece[:8] + carried[8 * x : 8 * x + 8]
+                piece = jnp.concatenate([head, piece[8:]], 0)
+            sums[f, x, group * SPAN : (group + 1) * SPAN, :] = piece
+        carried = turned[5 * SPAN :]
+
+
+def fill_faces(grid, f, second_half, gas, sums, up, down, row):
     ny = grid.span_y
-    for f in range(FIELDS):
-        up[f] = sums[f, 4]
-        down[f, :ny] = COUPLE * sums[f, 0, :ny] + gas[f, 0]
-        down[f, ny:] = COUPLE * sums[f, 0, ny:]
-        for x in range(5):
-            low_row = COUPLE * sums[f, x, 0:1, :]
-            if x < 4:
-                low_row = low_row + gas[f, x, 0:1, :]
-            high_row = COUPLE * sums[f, x, ny : ny + 1, :]
-            row[x, f : f + 1, :] = jnp.where(second_half, low_row, high_row)
+    up[f] = sums[f, 4]
+    down[f, :ny] = COUPLE * sums[f, 0, :ny] + gas[f, 0]
+    down[f, ny:] = COUPLE * sums[f, 0, ny:]
     for x in range(5):
-        row[x, FIELDS:, :] = jnp.zeros((8 - FIELDS, grid.span_z), F32)
+        low_row = COUPLE * sums[f, x, 0:1, :]
+        if x < 4:
+            low_row = low_row + gas[f, x, 0:1, :]
+        high_row = COUPLE * sums[f, x, ny : ny + 1, :]
+        row[x, f : f + 1, :] = jnp.where(second_half, low_row, high_row)
 
 
 def sample_kernel(
     grid, last, bricks, place, stay, lower, upper, gas, sums, from_up, from_down,
-    from_row, corner_low, corner_high, source, sampled, field, held
+    from_row, corner_low, corner_high, weights, source, sampled, field, held
 ):
     ny = grid.span_y
     second_half = place[1] == 1
@@ -308,7 +334,9 @@
             for i in range(UNROLL):
                 at = turn * UNROLL + i
                 block = part[:, pl.ds(pl.multiple_of(at * LANES, LANES), LANES)]
-                values = sample_block(grid, block, bricks[offset + at], held)
+                place_at = pl.multiple_of((offset + at) * 2 * LANES, 2 * LANES)
+                plane = weights[pl.ds(place_at, 2 * LANES), :]
+                values = sample_block(grid, block, bricks[offset + at], plane, held)
                 lanes = pl.ds(pl.multiple_of((offset + at) * LANES, LANES), LANES)
                 sampled[:, lanes] = values.astype(BF16)
             return carry
@@ -325,7 +353,7 @@
     return lax.ppermute(block, ("axial", "radial"), route)
 
 
-BIG = pltpu.CompilerParams(vmem_limit_bytes=24 * 2**20)
+BIG = pltpu.CompilerParams(vmem_limit_bytes=12 * 2**20)
 
 
 def deposit_stay_call(grid, bricks, stay):
@@ -339,25 +367,22 @@
     )(bricks, stay)
 
 
-def deposit_moved_call(grid, bricks, place, lower, upper, held, gas):
-    plane = jax.ShapeDtypeStruct((FIELDS, grid.pad_y, grid.span_z), F32)
+def deposit_moved_call(grid, bricks, lower, upper, held):
     return pl.pallas_call(
         functools.partial(deposit_moved_kernel, grid),
-        out_shape=(
-            jax.ShapeDtypeStruct((FIELDS, 5, grid.pad_y, grid.span_z), F32),
-            plane,
-            plane,
-            jax.ShapeDtypeStruct((5, 8, grid.span_z), F32),
-        ),
-        in_specs=[SMEM, SMEM, VMEM, VMEM, VMEM, VMEM],
-        scratch_shapes=[pltpu.VMEM((grid.rows, LANES), F32)],
+        out_shape=jax.ShapeDtypeStruct((grid.rows, LANES), F32),
+        in_specs=[SMEM, VMEM, VMEM, VMEM],
         compiler_params=BIG,
         name="deposit_moved",
-    )(bricks, place, lower, upper, held, gas)
+    )(bricks, lower, upper, held)
+
+
+WEIGHT_UNROLL = 8
 
 
 def exchange_kernel(
-    last, up, down, edge, from_up, from_down, from_row, corner_low, corner_high, sent, got
+    grid, last, bricks, stay, lower, upper, gas, total, sums, from_up, from_down, from_row,
+    corner_low, corner_high, weights, up, down, edge, sent, got
 ):
     a = lax.axis_index("axial")
     r = lax.axis_index("radial")
@@ -384,7 +409,6 @@
         greet(a - 1, 1 - r)
 
     peers = 1 + 2 * has_above.astype(jnp.int32) + 2 * has_below.astype(jnp.int32)
-    pl.semaphore_wait(barrier, peers)
 
     def copy(number, source, target, axial_at, radial_at):
         return pltpu.make_async_remote_copy(
@@ -394,26 +418,38 @@
         )
 
     row = copy(0, edge, from_row, a, 1 - r)
-    above = (
-        copy(1, up, from_up, a + 1, r),
-        copy(2, edge.at[4], corner_low, a + 1, 1 - r),
-    )
-    below = (
-        copy(3, down, from_down, a - 1, r),
-        copy(4, edge.at[0], corner_high, a - 1, 1 - r),
-    )
+    corner_up = copy(1, edge.at[4], corner_low, a + 1, 1 - r)
+    corner_down = copy(2, edge.at[0], corner_high, a - 1, 1 - r)
+    faces_up = [copy(3 + f, up.at[f], from_up.at[f], a + 1, r) for f in range(FIELDS)]
+    faces_down = [
+        copy(3 + FIELDS + f, down.at[f], from_down.at[f], a - 1, r) for f in range(FIELDS)
+    ]
+    select = merge_selector()
+    for x in range(5):
+        edge[x, FIELDS:, :] = jnp.zeros((8 - FIELDS, grid.span_z), F32)
+    for f in range(FIELDS):
+        merge_field(grid, f, select, total, sums)
+        fill_faces(grid, f, r == 1, gas, sums, up, down, edge)
+        if f == 0:
+            pl.semaphore_wait(barrier, peers)
+
+        @pl.when(has_above)
+        def _(f=f):
+            faces_up[f].start()
+
+        @pl.when(has_below)
+        def _(f=f):
+            faces_down[f].start()
+
+    row.start()
 
     @pl.when(has_above)
     def _():
-        for each in above:
-            each.start()
+        corner_up.start()
 
     @pl.when(has_below)
     def _():
-        for each in below:
-            each.start()
-
-    row.start()
+        corner_down.start()
 
     @pl.when(jnp.logical_not(has_below))
     def _():
@@ -425,42 +461,70 @@
         from_down[...] = jnp.zeros_like(from_down)
         corner_high[...] = jnp.zeros_like(corner_high)
 
+    offset = 0
+    for part in (stay, lower, upper):
+        blocks = part.shape[1] // LANES
+
+        def step(turn, carry, part=part, offset=offset):
+            for i in range(WEIGHT_UNROLL):
+                at = turn * WEIGHT_UNROLL + i
+                block = part[:, pl.ds(pl.multiple_of(at * LANES, LANES), LANES)]
+                _, shift_y = grid.place(bricks[offset + at])
+                both = jnp.concatenate(plane_weights(block, shift_y), 0)
+                place_at = pl.multiple_of((offset + at) * 2 * LANES, 2 * LANES)
+                weights[pl.ds(place_at, 2 * LANES), :] = both.astype(BF16)
+            return carry
+
+        lax.fori_loop(0, blocks // WEIGHT_UNROLL, step, 0)
+        offset += blocks
+
     row.wait()
 
     @pl.when(has_above)
     def _():
-        for each in above:
+        for each in faces_up + [corner_up]:
             each.wait_send()
-        for each in below:
+        for each in faces_down + [corner_down]:
             each.wait_recv()
 
     @pl.when(has_below)
     def _():
-        for each in below:
+        for each in faces_down + [corner_down]:
             each.wait_send()
-        for each in above:
+        for each in faces_up + [corner_up]:
             each.wait_recv()
 
 
-def exchange_call(last, up, down, edge):
-    corner = jax.ShapeDtypeStruct(edge.shape[1:], F32)
+def exchange_call(grid, last, bricks, stay, lower, upper, gas, total):
+    plane = (FIELDS, grid.pad_y, grid.span_z)
+    edge = (5, 8, grid.span_z)
+    corner = jax.ShapeDtypeStruct(edge[1:], F32)
+    copies = 3 + 2 * FIELDS
     return pl.pallas_call(
-        functools.partial(exchange_kernel, last),
+        functools.partial(exchange_kernel, grid, last),
         out_shape=(
-            jax.ShapeDtypeStruct(up.shape, F32),
-            jax.ShapeDtypeStruct(down.shape, F32),
-            jax.ShapeDtypeStruct(edge.shape, F32),
+            jax.ShapeDtypeStruct((FIELDS, 5, grid.pad_y, grid.span_z), F32),
+            jax.ShapeDtypeStruct(plane, F32),
+            jax.ShapeDtypeStruct(plane, F32),
+            jax.ShapeDtypeStruct(edge, F32),
             corner,
             corner,
+            jax.ShapeDtypeStruct((bricks.shape[0] * 2 * LANES, LANES), BF16),
         ),
-        in_specs=[VMEM] * 3,
-        out_specs=(VMEM,) * 5,
-        scratch_shapes=[pltpu.SemaphoreType.DMA((5,)), pltpu.SemaphoreType.DMA((5,))],
+        in_specs=[SMEM] + [VMEM] * 5,
+        out_specs=(VMEM,) * 7,
+        scratch_shapes=[
+            pltpu.VMEM(plane, F32),
+            pltpu.VMEM(plane, F32),
+            pltpu.VMEM(edge, F32),
+            pltpu.SemaphoreType.DMA((copies,)),
+            pltpu.SemaphoreType.DMA((copies,)),
+        ],
         compiler_params=pltpu.CompilerParams(
-            collective_id=0, has_side_effects=True, vmem_limit_bytes=4 * 2**20
+            collective_id=0, has_side_effects=True, vmem_limit_bytes=8 * 2**20
         ),
         name="exchange",
-    )(up, down, edge)
+    )(bricks, stay, lower, upper, gas, total)
 
 
 def sample_call(grid, last, bricks, place, *arrays):
@@ -471,7 +535,7 @@
             jax.ShapeDtypeStruct(gas.shape, F32),
             jax.ShapeDtypeStruct((FIELDS, bricks.shape[0] * LANES), BF16),
         ),
-        in_specs=[SMEM, SMEM] + [VMEM] * 10,
+        in_specs=[SMEM, SMEM] + [VMEM] * 11,
         scratch_shapes=[
             pltpu.VMEM((FIELDS, 5, grid.pad_y, grid.span_z), F32),
             pltpu.VMEM((grid.rows, LANES), F32),
@@ -496,16 +560,14 @@
             if 0 <= a + step_a < axial
         ]
 
-    up, down, stay = gather_call(load, offset, cell, rows)
+    up, down, stay, bricks = gather_call(load, offset, cell, rows, bricks)
     lower = shift(up, route(1, False))
     upper = shift(down, route(-1, False))
     held = deposit_stay_call(grid, bricks, stay)
-    sums, plane_up, plane_down, edge = deposit_moved_call(
-        grid, bricks, place, lower, upper, held, gas
-    )
-    arrived = exchange_call(axial - 1, plane_up, plane_down, edge)
+    total = deposit_moved_call(grid, bricks, lower, upper, held)
+    arrived = exchange_call(grid, axial - 1, bricks, stay, lower, upper, gas, total)
     return sample_call(
-        grid, axial - 1, bricks, place, stay, lower, upper, gas, sums, *arrived
+        grid, axial - 1, bricks, place, stay, lower, upper, gas, *arrived
     )
 
 

time: 57.1 us -> 56.9 us (level)
    pallas_call x1, Pallas kernels: 9.36 us -> 8.06 us  [sample_call(): pl.pallas_call(functools.partial(sample_kernel, grid, last), out_shape=(j...]
    pallas_call x2, Pallas kernels: 24.2 us -> 24.8 us  [the longest x1 20.9 us: exchange_call(): pl.pallas_call(functools.partial(exchange_kernel, grid, last), out_shape=...]
    unnamed x14 -> x12, local copies, waits for them, and re-layouts: 4.34 us -> 4.34 us
where the time goes in v2:
time: 56.9 us; the launch traced here: 56.4 us
  Pallas kernels  40.9 us (72%)
  starting transfers between devices  10.4 us (18%)
  local copies, waits for them, and re-layouts  4.34 us (8%)
  between operations  0.71 us (1%)
    pallas_call x1, Pallas kernels, exchange_call(): pl.pallas_call(functools.partial(exchange_kernel, grid, last), out_shape=...  20.9 us
    ppermute x2, starting transfers between devices, shift(): return lax.ppermute(block, ('axial', 'radial'), route)  10.4 us
    pallas_call x1, Pallas kernels, sample_call(): pl.pallas_call(functools.partial(sample_kernel, grid, last), out_shape=(j...  8.06 us
    unnamed x12, local copies, waits for them, and re-layouts  4.34 us
    pallas_call x1, Pallas kernels, gather_call(): pl.pallas_call(gather_kernel, out_shape=(moved, moved, jax.ShapeDtypeStru...  4.16 us
    pallas_call x1, Pallas kernels, deposit_moved_call(): pl.pallas_call(functools.partial(deposit_moved_kernel, grid), out_shape=j...  3.9 us
    pallas_call x1, Pallas kernels, deposit_stay_call(): pl.pallas_call(functools.partial(deposit_stay_kernel, grid), out_shape=ja...  3.86 us
  transfers between devices with their start and end apart: 2, of which 0 were waited for; matrix products, arithmetic and copies ran while one was open for 0% of the time, Pallas kernels for 7%

profile of v2, /device:TPU:2, one launch (start us, length us, event | category | flops | bytes accessed | tf_op | source)
XLA Modules:
  0.0 56.4 jit_solution(12459877311973686740)
XLA Ops:
  0.6 0.0 copy-start.1
  0.6 1.0 %copy-done.1 = f32[5,16384]{1,0:T(8,128)S(1)} copy-done((f32[5,16384]{1,0:T(8,128)S(1)}, f32[5,16384]{1,0:T(8,128)}, u32[]{:S(2)}) %copy-start.1) | copy-done | bytes 327704
  1.7 0.0 copy-start.2
  1.7 0.9 %copy-done.2 = f32[3,16384]{1,0:T(4,128)S(1)} copy-done((f32[3,16384]{1,0:T(4,128)S(1)}, f32[3,16384]{1,0:T(4,128)}, u32[]{:S(2)}) %copy-start.2) | copy-done | bytes 196632
  2.6 0.0 copy-start.3
  2.6 0.8 %copy-done.3 = s32[16384]{0:T(1024)S(1)} copy-done((s32[16384]{0:T(1024)S(1)}, s32[16384]{0:T(1024)}, u32[]{:S(2)}) %copy-start.3) | copy-done | bytes 65560
  3.5 0.0 copy-start.4
  3.5 0.8 %copy-done.4 = s32[2,8192]{1,0:T(2,128)S(1)} copy-done((s32[2,8192]{1,0:T(2,128)S(1)}, s32[2,8192]{1,0:T(2,128)}, u32[]{:S(2)}) %copy-start.4) | copy-done | bytes 65560
  4.3 0.0 copy-start.5
  4.3 0.7 %copy-done.5 = s32[256]{0:T(256)S(1)} copy-done((s32[256]{0:T(256)S(1)}, s32[256]{0:T(256)}, u32[]{:S(2)}) %copy-start.5) | copy-done | bytes 1048
  5.0 4.2 %gather_rows.1 = (f32[8,8192]{1,0:T(8,128)S(1)}, f32[8,8192]{1,0:T(8,128)S(1)}, f32[8,16384]{1,0:T(8,128)S(1)}, s32[256]{0:T(256)S(1)}) custom-call(f32[5,16384]{1,0:T(8,128)S(1)} %copy-done.1, f32[3,16384]{1,0:T(4,128)S(1)} %copy-done.2, s32[1,16384]{1,0:T(1,128)S(1)} %bitcast.3, s32[2,8192]{1,0:T(2,128)S(1)} %copy-done.4, s32[256]{0:T(256)S(1)} %copy-done.5), custom_call_target="tpu_custom_call" | custom-call | tf_op jit(solution)/shard_map/gather_rows/pallas_call | solution.py:118
  9.2 1.9 %collective-permute-start = (f32[8,8192]{1,0:T(8,128)S(1)}, f32[8,8192]{1,0:T(8,128)S(1)}, u32[]{:S(2)}, u32[]{:S(2)}) collective-permute-start(f32[8,8192]{1,0:T(8,128)S(1)} %get-tuple-element.15), channel_id=1, source_target_pairs={{0,2},{1,3},{2,4},{3,5},{4,6},{5,7},{6,8},{7,9},{8,10},{9,11},{10,... | collective-permute-start | bytes 786440 | tf_op jit(solution)/shard_map/ppermute | solution.py:353
  11.1 8.4 %collective-permute-start.1 = (f32[8,8192]{1,0:T(8,128)S(1)}, f32[8,8192]{1,0:T(8,128)S(1)}, u32[]{:S(2)}, u32[]{:S(2)}) collective-permute-start(f32[8,8192]{1,0:T(8,128)S(1)} %get-tuple-element.16), channel_id=1, source_target_pairs={{2,0},{3,1},{4,2},{5,3},{6,4},{7,5},{8,6},{9,7},{10,8},{11,9},{12,... | collective-permute-start | bytes 786440 | tf_op jit(solution)/shard_map/ppermute | solution.py:353
  19.5 3.9 %deposit_stay.1.held = f32[3960,128]{1,0:T(8,128)S(1)} custom-call(s32[256]{0:T(256)S(1)} %get-tuple-element.13.bricks, f32[8,16384]{1,0:T(8,128)S(1)} %get-tuple-element.14.parcels.stay), custom_call_target="tpu_custom_call" | custom-call | flops 1000000000 | bytes 10000000 | tf_op jit(solution)/shard_map/deposit_stay/pallas_call | solution.py:360
  23.4 0.1 pad_add_fusion.place
  23.5 0.0 copy-start
  23.5 0.0 collective-permute-done.lower
  23.5 0.0 collective-permute-done.1.upper
  23.5 3.9 %deposit_moved.1.total = f32[3960,128]{1,0:T(8,128)S(1)} custom-call(s32[256]{0:T(256)S(1)} %get-tuple-element.13.bricks, f32[8,8192]{1,0:T(8,128)S(1)} %collective-permute-done.lower, f32[8,8192]{1,0:T(8,128)S(1)} %collective-permute-done.1.upper, f32[3960,128]{1,0:T(8,128)S(1)} %deposit_stay.1.held), custom_call_target="tpu_custom_call" | custom-call | tf_op jit(solution)/shard_map/deposit_moved/pallas_call | solution.py:371
  27.4 0.0 copy-done
  27.4 20.9 %exchange.1 = (f32[5,5,72,256]{3,2,1,0:T(8,128)S(1)}, f32[5,72,256]{2,1,0:T(8,128)S(1)}, f32[5,72,256]{2,1,0:T(8,128)S(1)}, f32[5,8,256]{2,1,0:T(8,128)S(1)}, f3...) custom-call(s32[256]{0:T(256)S(1)} %get-tuple-element.13.bricks, ...), custom_call_target="tpu_custom_call" | custom-call | tf_op jit(solution)/shard_map/exchange/pallas_call | solution.py:503
  48.4 8.1 %sample.1 = (f32[5,4,64,256]{3,2,1,0:T(8,128)}, bf16[5,32768]{1,0:T(8,128)(2,1)}) custom-call(s32[256]{0:T(256)S(1)} %get-tuple-element.13.bricks, s32[2]{0:T(128)S(1)} %pad_add_fusion.place, f32[8,16384]{1,0:T(8,128)S(1)} %get-tuple-element.14.parcels.stay, f32[8,8192]{1,0:T(8,128)S(1)} %collective-permute-done.lower, ...), custom_call_target="tpu_custom_call" | custom-call | tf_op jit(solution)/shard_map/sample/pallas_call | solution.py:532
Async XLA Ops:
  0.6 1.0 %copy-start.1 = (f32[5,16384]{1,0:T(8,128)S(1)}, f32[5,16384]{1,0:T(8,128)}, u32[]{:S(2)}) copy-start(f32[5,16384]{1,0:T(8,128)} %load_in.1) | copy-start | bytes 983044
  1.7 0.9 %copy-start.2 = (f32[3,16384]{1,0:T(4,128)S(1)}, f32[3,16384]{1,0:T(4,128)}, u32[]{:S(2)}) copy-start(f32[3,16384]{1,0:T(4,128)} %offset_in.1) | copy-start | bytes 589828
  2.6 0.8 %copy-start.3 = (s32[16384]{0:T(1024)S(1)}, s32[16384]{0:T(1024)}, u32[]{:S(2)}) copy-start(s32[16384]{0:T(1024)} %param.8) | copy-start | bytes 196612
  3.5 0.8 %copy-start.4 = (s32[2,8192]{1,0:T(2,128)S(1)}, s32[2,8192]{1,0:T(2,128)}, u32[]{:S(2)}) copy-start(s32[2,8192]{1,0:T(2,128)} %rows_in.1) | copy-start | bytes 196612
  4.3 0.7 %copy-start.5 = (s32[256]{0:T(256)S(1)}, s32[256]{0:T(256)}, u32[]{:S(2)}) copy-start(s32[256]{0:T(256)} %bricks_in.1) | copy-start | bytes 3076
  9.2 14.3 %collective-permute-start = (f32[8,8192]{1,0:T(8,128)S(1)}, f32[8,8192]{1,0:T(8,128)S(1)}, u32[]{:S(2)}, u32[]{:S(2)}) collective-permute-start(f32[8,8192]{1,0:T(8,128)S(1)} %get-tuple-element.15), channel_id=1, source_target_pairs={{0,2},{1,3},{2,4},{3,5},{4,6},{5,7},{6,8},{7,9},{8,10},{9,11},{10,... | collective-permute-start | bytes 786440 | tf_op jit(solution)/shard_map/ppermute | solution.py:353
  11.1 12.4 %collective-permute-start.1 = (f32[8,8192]{1,0:T(8,128)S(1)}, f32[8,8192]{1,0:T(8,128)S(1)}, u32[]{:S(2)}, u32[]{:S(2)}) collective-permute-start(f32[8,8192]{1,0:T(8,128)S(1)} %get-tuple-element.16), channel_id=1, source_target_pairs={{2,0},{3,1},{4,2},{5,3},{6,4},{7,5},{8,6},{9,7},{10,8},{11,9},{12,... | collective-permute-start | bytes 786440 | tf_op jit(solution)/shard_map/ppermute | solution.py:353
  23.5 3.9 %copy-start = (f32[5,4,64,256]{3,2,1,0:T(8,128)S(1)}, f32[5,4,64,256]{3,2,1,0:T(8,128)}, u32[]{:S(2)}) copy-start(f32[5,4,64,256]{3,2,1,0:T(8,128)} %gas.3) | copy-start | bytes 3932164

commit v3 on v2

--- a/solution.py
+++ b/solution.py
@@ -179,14 +179,17 @@
     return jnp.concatenate([both, both], 1)
 
 
-def deposit_block(grid, block, brick, total):
-    first, shift_y = grid.place(brick)
-    high, low = plane_weights(block, shift_y)
+def spread_block(block, weights):
+    high, low = weights
     plane = jnp.concatenate([high.astype(BF16), low.astype(BF16)], 1)
     depth = depth_weights(block)
     loads = jnp.concatenate([block[f : f + 1] * depth for f in range(FIELDS)], 0)
     both = lax.dot_general(doubled(loads), plane, NT, preferred_element_type=F32)
-    summed = both[: 8 * FIELDS] + both[8 * FIELDS :]
+    return both[: 8 * FIELDS] + both[8 * FIELDS :]
+
+
+def add_block(grid, summed, brick, total):
+    first, _ = grid.place(brick)
     for f in range(FIELDS):
         rows = pl.ds(first + f * grid.rows_z, 8)
         total[rows, :] += summed[8 * f : 8 * f + 8]
@@ -212,28 +215,27 @@
 UNROLL = 32
 
 
-def deposit_loop(grid, parcels, bricks, offset, count, total):
-    def step(turn, carry):
-        for i in range(UNROLL):
-            at = turn * UNROLL + i
-            block = parcels[:, pl.ds(pl.multiple_of(at * LANES, LANES), LANES)]
-            deposit_block(grid, block, bricks[offset + at], total)
-        return carry
-
-    lax.fori_loop(0, count // UNROLL, step, 0)
-
-
-def deposit_stay_kernel(grid, bricks, parcels, total):
+def deposit_kernel(grid, bricks, spread, lower, upper, total):
     total[...] = jnp.zeros_like(total)
-    deposit_loop(grid, parcels, bricks, 0, parcels.shape[1] // LANES, total)
-
-
-def deposit_moved_kernel(grid, bricks, lower, upper, held, total):
-    total[...] = held[...]
     blocks = lower.shape[1] // LANES
-    start = bricks.shape[0] - 2 * blocks
-    deposit_loop(grid, lower, bricks, start, blocks, total)
-    deposit_loop(grid, upper, bricks, start + blocks, blocks, total)
+    resident = bricks.shape[0] - 2 * blocks
+    ratio = resident // (2 * blocks)
+    for part, offset in ((lower, 0), (upper, blocks)):
+
+        def step(turn, carry, part=part, offset=offset):
+            for i in range(UNROLL):
+                at = turn * UNROLL + i
+                block = part[:, pl.ds(pl.multiple_of(at * LANES, LANES), LANES)]
+                brick = bricks[resident + offset + at]
+                weights = plane_weights(block, grid.place(brick)[1])
+                add_block(grid, spread_block(block, weights), brick, total)
+                for j in range(ratio):
+                    own = (offset + at) * ratio + j
+                    rows = pl.ds(pl.multiple_of(own * 8 * FIELDS, 8), 8 * FIELDS)
+                    add_block(grid, spread[rows, :], bricks[own], total)
+            return carry
+
+        lax.fori_loop(0, blocks // UNROLL, step, 0)
 
 
 def merge_selector():
@@ -277,12 +279,12 @@
 
 
 def sample_kernel(
-    grid, last, bricks, place, stay, lower, upper, gas, sums, from_up, from_down,
+    grid, last, bricks, stay, lower, upper, gas, sums, from_up, from_down,
     from_row, corner_low, corner_high, weights, source, sampled, field, held
 ):
     ny = grid.span_y
-    second_half = place[1] == 1
-    at_end = place[0] == last
+    second_half = lax.axis_index("radial") == 1
+    at_end = lax.axis_index("axial") == last
     face = jnp.where(second_half, 1.0, 0.0)
     for f in range(FIELDS):
         for x in range(5):
@@ -349,35 +351,119 @@
 VMEM = pl.BlockSpec(memory_space=pltpu.VMEM)
 
 
-def shift(block, route):
-    return lax.ppermute(block, ("axial", "radial"), route)
-
-
 BIG = pltpu.CompilerParams(vmem_limit_bytes=12 * 2**20)
 
 
-def deposit_stay_call(grid, bricks, stay):
+def deposit_call(grid, bricks, spread, lower, upper):
     return pl.pallas_call(
-        functools.partial(deposit_stay_kernel, grid),
-        out_shape=jax.ShapeDtypeStruct((grid.rows, LANES), F32),
-        in_specs=[SMEM, VMEM],
-        compiler_params=BIG,
-        cost_estimate=pl.CostEstimate(flops=10**9, bytes_accessed=10**7, transcendentals=0),
-        name="deposit_stay",
-    )(bricks, stay)
-
-
-def deposit_moved_call(grid, bricks, lower, upper, held):
-    return pl.pallas_call(
-        functools.partial(deposit_moved_kernel, grid),
+        functools.partial(deposit_kernel, grid),
         out_shape=jax.ShapeDtypeStruct((grid.rows, LANES), F32),
         in_specs=[SMEM, VMEM, VMEM, VMEM],
         compiler_params=BIG,
-        name="deposit_moved",
-    )(bricks, lower, upper, held)
-
-
-WEIGHT_UNROLL = 8
+        name="deposit",
+    )(bricks, spread, lower, upper)
+
+
+def signal_entry(axial_at, radial_at):
+    pl.semaphore_signal(
+        pltpu.get_barrier_semaphore(), inc=1, device_id=(axial_at, radial_at),
+        device_id_type=pl.DeviceIdType.MESH,
+    )
+
+
+def store_weights(target, at, weights):
+    place = pl.multiple_of(at * 2 * LANES, 2 * LANES)
+    target[pl.ds(place, 2 * LANES), :] = jnp.concatenate(weights, 0).astype(BF16)
+
+
+FILLER = 1
+
+
+def migrate_kernel(
+    grid, last, bricks, up, down, stay, lower, upper, spread, sent, got
+):
+    a = lax.axis_index("axial")
+    r = lax.axis_index("radial")
+    has_above = a < last
+    has_below = a > 0
+
+    @pl.when(has_above)
+    def _():
+        signal_entry(a + 1, r)
+
+    @pl.when(has_below)
+    def _():
+        signal_entry(a - 1, r)
+
+    def copy(number, source, target, axial_at):
+        return pltpu.make_async_remote_copy(
+            src_ref=source, dst_ref=target, send_sem=sent.at[number],
+            recv_sem=got.at[number], device_id=(axial_at, r),
+            device_id_type=pl.DeviceIdType.MESH,
+        )
+
+    rising = copy(0, up, lower, a + 1)
+    falling = copy(1, down, upper, a - 1)
+
+    def step(turn, carry):
+        for i in range(UNROLL):
+            at = turn * UNROLL + i
+            block = stay[:, pl.ds(pl.multiple_of(at * LANES, LANES), LANES)]
+            plane = plane_weights(block, grid.place(bricks[at])[1])
+            rows = pl.ds(pl.multiple_of(at * 8 * FIELDS, 8), 8 * FIELDS)
+            spread[rows, :] = spread_block(block, plane)
+        return carry
+
+    lax.fori_loop(0, FILLER, step, 0)
+    peers = has_above.astype(jnp.int32) + has_below.astype(jnp.int32)
+    pl.semaphore_wait(pltpu.get_barrier_semaphore(), peers)
+
+    @pl.when(has_above)
+    def _():
+        rising.start()
+
+    @pl.when(has_below)
+    def _():
+        falling.start()
+
+    @pl.when(jnp.logical_not(has_below))
+    def _():
+        lower[...] = jnp.zeros_like(lower)
+
+    @pl.when(jnp.logical_not(has_above))
+    def _():
+        upper[...] = jnp.zeros_like(upper)
+
+    lax.fori_loop(FILLER, stay.shape[1] // LANES // UNROLL, step, 0)
+
+    @pl.when(has_above)
+    def _():
+        rising.wait_send()
+        falling.wait_recv()
+
+    @pl.when(has_below)
+    def _():
+        falling.wait_send()
+        rising.wait_recv()
+
+
+def migrate_call(grid, last, bricks, up, down, stay):
+    blocks = stay.shape[1] // LANES
+    return pl.pallas_call(
+        functools.partial(migrate_kernel, grid, last),
+        out_shape=(
+            jax.ShapeDtypeStruct(up.shape, F32),
+            jax.ShapeDtypeStruct(down.shape, F32),
+            jax.ShapeDtypeStruct((blocks * 8 * FIELDS, LANES), F32),
+        ),
+        in_specs=[SMEM] + [VMEM] * 3,
+        out_specs=(VMEM,) * 3,
+        scratch_shapes=[pltpu.SemaphoreType.DMA((2,)), pltpu.SemaphoreType.DMA((2,))],
+        compiler_params=pltpu.CompilerParams(
+            collective_id=1, has_side_effects=True, vmem_limit_bytes=8 * 2**20
+        ),
+        name="migrate",
+    )(bricks, up, down, stay)
 
 
 def exchange_kernel(
@@ -388,25 +474,17 @@
     r = lax.axis_index("radial")
     has_above = a < last
     has_below = a > 0
-    barrier = pltpu.get_barrier_semaphore()
-
-    def greet(axial_at, radial_at):
-        pl.semaphore_signal(
-            barrier, inc=1, device_id=(axial_at, radial_at),
-            device_id_type=pl.DeviceIdType.MESH,
-        )
-
-    greet(a, 1 - r)
+    signal_entry(a, 1 - r)
 
     @pl.when(has_above)
     def _():
-        greet(a + 1, r)
-        greet(a + 1, 1 - r)
+        signal_entry(a + 1, r)
+        signal_entry(a + 1, 1 - r)
 
     @pl.when(has_below)
     def _():
-        greet(a - 1, r)
-        greet(a - 1, 1 - r)
+        signal_entry(a - 1, r)
+        signal_entry(a - 1, 1 - r)
 
     peers = 1 + 2 * has_above.astype(jnp.int32) + 2 * has_below.astype(jnp.int32)
 
@@ -427,11 +505,23 @@
     select = merge_selector()
     for x in range(5):
         edge[x, FIELDS:, :] = jnp.zeros((8 - FIELDS, grid.span_z), F32)
+    def weigh(part, offset):
+        def step(turn, carry):
+            for i in range(UNROLL):
+                at = turn * UNROLL + i
+                block = part[:, pl.ds(pl.multiple_of(at * LANES, LANES), LANES)]
+                plane = plane_weights(block, grid.place(bricks[offset + at])[1])
+                store_weights(weights, offset + at, plane)
+            return carry
+
+        lax.fori_loop(0, part.shape[1] // LANES // UNROLL, step, 0)
+
     for f in range(FIELDS):
         merge_field(grid, f, select, total, sums)
         fill_faces(grid, f, r == 1, gas, sums, up, down, edge)
-        if f == 0:
-            pl.semaphore_wait(barrier, peers)
+    weigh(stay, 0)
+    pl.semaphore_wait(pltpu.get_barrier_semaphore(), peers)
+    for f in range(FIELDS):
 
         @pl.when(has_above)
         def _(f=f):
@@ -461,23 +551,9 @@
         from_down[...] = jnp.zeros_like(from_down)
         corner_high[...] = jnp.zeros_like(corner_high)
 
-    offset = 0
-    for part in (stay, lower, upper):
-        blocks = part.shape[1] // LANES
-
-        def step(turn, carry, part=part, offset=offset):
-            for i in range(WEIGHT_UNROLL):
-                at = turn * WEIGHT_UNROLL + i
-                block = part[:, pl.ds(pl.multiple_of(at * LANES, LANES), LANES)]
-                _, shift_y = grid.place(bricks[offset + at])
-                both = jnp.concatenate(plane_weights(block, shift_y), 0)
-                place_at = pl.multiple_of((offset + at) * 2 * LANES, 2 * LANES)
-                weights[pl.ds(place_at, 2 * LANES), :] = both.astype(BF16)
-            return carry
-
-        lax.fori_loop(0, blocks // WEIGHT_UNROLL, step, 0)
-        offset += blocks
-
+    resident = stay.shape[1] // LANES
+    weigh(lower, resident)
+    weigh(upper, resident + lower.shape[1] // LANES)
     row.wait()
 
     @pl.when(has_above)
@@ -527,7 +603,7 @@
     )(bricks, stay, lower, upper, gas, total)
 
 
-def sample_call(grid, last, bricks, place, *arrays):
+def sample_call(grid, last, bricks, *arrays):
     gas = arrays[3]
     return pl.pallas_call(
         functools.partial(sample_kernel, grid, last),
@@ -535,39 +611,26 @@
             jax.ShapeDtypeStruct(gas.shape, F32),
             jax.ShapeDtypeStruct((FIELDS, bricks.shape[0] * LANES), BF16),
         ),
-        in_specs=[SMEM, SMEM] + [VMEM] * 11,
+        in_specs=[SMEM] + [VMEM] * 11,
         scratch_shapes=[
             pltpu.VMEM((FIELDS, 5, grid.pad_y, grid.span_z), F32),
             pltpu.VMEM((grid.rows, LANES), F32),
         ],
         compiler_params=BIG,
         name="sample",
-    )(bricks, place, *arrays)
+    )(bricks, *arrays)
 
 
 def per_device(load, offset, cell, rows, bricks, gas):
     axial = lax.axis_size("axial")
-    radial = lax.axis_size("radial")
     span_y, span_z = gas.shape[2], gas.shape[3]
     grid = Grid(span_y, span_z)
-    place = jnp.stack([lax.axis_index("axial"), lax.axis_index("radial")]).astype(jnp.int32)
-    everyone = [(a, r) for a in range(axial) for r in range(radial)]
-
-    def route(step_a, flip):
-        return [
-            (a * radial + r, (a + step_a) * radial + (radial - 1 - r if flip else r))
-            for a, r in everyone
-            if 0 <= a + step_a < axial
-        ]
-
     up, down, stay, bricks = gather_call(load, offset, cell, rows, bricks)
-    lower = shift(up, route(1, False))
-    upper = shift(down, route(-1, False))
-    held = deposit_stay_call(grid, bricks, stay)
-    total = deposit_moved_call(grid, bricks, lower, upper, held)
+    lower, upper, spread = migrate_call(grid, axial - 1, bricks, up, down, stay)
+    total = deposit_call(grid, bricks, spread, lower, upper)
     arrived = exchange_call(grid, axial - 1, bricks, stay, lower, upper, gas, total)
     return sample_call(
-        grid, axial - 1, bricks, place, stay, lower, upper, gas, *arrived
+        grid, axial - 1, bricks, stay, lower, upper, gas, *arrived
     )
 
 

time: 56.9 us -> 52.9 us (0.930)
  starting transfers between devices: 10.4 us -> 0 us
  Pallas kernels: 40.9 us -> 47.1 us
    ppermute x2 -> x0, starting transfers between devices: 10.4 us -> none  [shift(): return lax.ppermute(block, ('axial', 'radial'), route)]
    pallas_call x2, Pallas kernels: 7.76 us -> 17.5 us  [the longest x1 12.1 us: migrate_call(): pl.pallas_call(functools.partial(migrate_kernel, grid, last), out_shape=(...]
    pallas_call x1, Pallas kernels: 20.9 us -> 17.4 us  [exchange_call(): pl.pallas_call(functools.partial(exchange_kernel, grid, last), out_shape=...]
  transfers between devices with their start and end apart: 2 -> 0, of which waited for: 0 -> 0; matrix products, arithmetic and copies ran while one was open for 0% -> 0% of each run, Pallas kernels for 7% -> 0%
where the time goes in v3:
time: 52.9 us; the launch traced here: 52.1 us
  Pallas kernels  47.1 us (89%)
  local copies, waits for them, and re-layouts  4.35 us (8%)
  between operations  0.69 us (1%)
    pallas_call x1, Pallas kernels, exchange_call(): pl.pallas_call(functools.partial(exchange_kernel, grid, last), out_shape=...  17.4 us
    pallas_call x1, Pallas kernels, migrate_call(): pl.pallas_call(functools.partial(migrate_kernel, grid, last), out_shape=(...  12.1 us
    pallas_call x1, Pallas kernels, sample_call(): pl.pallas_call(functools.partial(sample_kernel, grid, last), out_shape=(j...  8 us
    pallas_call x1, Pallas kernels, deposit_call(): pl.pallas_call(functools.partial(deposit_kernel, grid), out_shape=jax.Sha...  5.47 us
    unnamed x12, local copies, waits for them, and re-layouts  4.35 us
    pallas_call x1, Pallas kernels, gather_call(): pl.pallas_call(gather_kernel, out_shape=(moved, moved, jax.ShapeDtypeStru...  4.15 us

profile of v3, /device:TPU:2, one launch (start us, length us, event | category | flops | bytes accessed | tf_op | source)
XLA Modules:
  0.0 52.1 jit_solution(6873707398078870551)
XLA Ops:
  0.6 0.0 copy-start.1
  0.6 1.0 %copy-done.1 = f32[5,16384]{1,0:T(8,128)S(1)} copy-done((f32[5,16384]{1,0:T(8,128)S(1)}, f32[5,16384]{1,0:T(8,128)}, u32[]{:S(2)}) %copy-start.1) | copy-done | bytes 327704
  1.7 0.0 copy-start.2
  1.7 0.9 %copy-done.2 = f32[3,16384]{1,0:T(4,128)S(1)} copy-done((f32[3,16384]{1,0:T(4,128)S(1)}, f32[3,16384]{1,0:T(4,128)}, u32[]{:S(2)}) %copy-start.2) | copy-done | bytes 196632
  2.6 0.0 copy-start.3
  2.6 0.8 %copy-done.3 = s32[16384]{0:T(1024)S(1)} copy-done((s32[16384]{0:T(1024)S(1)}, s32[16384]{0:T(1024)}, u32[]{:S(2)}) %copy-start.3) | copy-done | bytes 65560
  3.5 0.0 copy-start.4
  3.5 0.8 %copy-done.4 = s32[2,8192]{1,0:T(2,128)S(1)} copy-done((s32[2,8192]{1,0:T(2,128)S(1)}, s32[2,8192]{1,0:T(2,128)}, u32[]{:S(2)}) %copy-start.4) | copy-done | bytes 65560
  4.3 0.0 copy-start.5
  4.3 0.7 %copy-done.5 = s32[256]{0:T(256)S(1)} copy-done((s32[256]{0:T(256)S(1)}, s32[256]{0:T(256)}, u32[]{:S(2)}) %copy-start.5) | copy-done | bytes 1048
  5.0 4.1 %gather_rows.1 = (f32[8,8192]{1,0:T(8,128)S(1)}, f32[8,8192]{1,0:T(8,128)S(1)}, f32[8,16384]{1,0:T(8,128)S(1)}, s32[256]{0:T(256)S(1)}) custom-call(f32[5,16384]{1,0:T(8,128)S(1)} %copy-done.1, f32[3,16384]{1,0:T(4,128)S(1)} %copy-done.2, s32[1,16384]{1,0:T(1,128)S(1)} %bitcast.1, s32[2,8192]{1,0:T(2,128)S(1)} %copy-done.4, s32[256]{0:T(256)S(1)} %copy-done.5), custom_call_target="tpu_custom_call" | custom-call | tf_op jit(solution)/shard_map/gather_rows/pallas_call | solution.py:118
  9.1 12.1 %migrate.1 = (f32[8,8192]{1,0:T(8,128)S(1)}, f32[8,8192]{1,0:T(8,128)S(1)}, f32[5120,128]{1,0:T(8,128)S(1)}) custom-call(s32[256]{0:T(256)S(1)} %get-tuple-element.16.bricks, f32[8,8192]{1,0:T(8,128)S(1)} %get-tuple-element.18.up, f32[8,8192]{1,0:T(8,128)S(1)} %get-tuple-element.19.down, f32[8,16384]{1,0:T(8,128)S(1)} %get-tuple-element.17.stay), custom_call_target="tpu_custom_call" | custom-call | tf_op jit(solution)/shard_map/migrate/pallas_call | solution.py:452
  21.2 0.0 copy-start
  21.2 5.5 %deposit.1.total = f32[3960,128]{1,0:T(8,128)S(1)} custom-call(s32[256]{0:T(256)S(1)} %get-tuple-element.16.bricks, f32[5120,128]{1,0:T(8,128)S(1)} %get-tuple-element.22.spread, f32[8,8192]{1,0:T(8,128)S(1)} %get-tuple-element.20.lower, f32[8,8192]{1,0:T(8,128)S(1)} %get-tuple-element.21.upper), custom_call_target="tpu_custom_call" | custom-call | tf_op jit(solution)/shard_map/deposit/pallas_call | solution.py:358
  26.7 0.0 copy-done
  26.7 17.4 %exchange.1 = (f32[5,5,72,256]{3,2,1,0:T(8,128)S(1)}, f32[5,72,256]{2,1,0:T(8,128)S(1)}, f32[5,72,256]{2,1,0:T(8,128)S(1)}, f32[5,8,256]{2,1,0:T(8,128)S(1)}, f3...) custom-call(s32[256]{0:T(256)S(1)} %get-tuple-element.16.bricks, ...), custom_call_target="tpu_custom_call" | custom-call | tf_op jit(solution)/shard_map/exchange/pallas_call | solution.py:579
  44.1 8.0 %sample.1 = (f32[5,4,64,256]{3,2,1,0:T(8,128)}, bf16[5,32768]{1,0:T(8,128)(2,1)}) custom-call(s32[256]{0:T(256)S(1)} %get-tuple-element.16.bricks, f32[8,16384]{1,0:T(8,128)S(1)} %get-tuple-element.17.stay, f32[8,8192]{1,0:T(8,128)S(1)} %get-tuple-element.20.lower, f32[8,8192]{1,0:T(8,128)S(1)} %get-tuple-element.21.upper, f32[5,4,64,256]{3,2,1,0:T(8,128)S(1)} %copy-done, ...), custom_call_target="tpu_custom_call" | custom-call | tf_op jit(solution)/shard_map/sample/pallas_call | solution.py:608
Async XLA Ops:
  0.6 1.0 %copy-start.1 = (f32[5,16384]{1,0:T(8,128)S(1)}, f32[5,16384]{1,0:T(8,128)}, u32[]{:S(2)}) copy-start(f32[5,16384]{1,0:T(8,128)} %load_in.1) | copy-start | bytes 983044
  1.7 0.9 %copy-start.2 = (f32[3,16384]{1,0:T(4,128)S(1)}, f32[3,16384]{1,0:T(4,128)}, u32[]{:S(2)}) copy-start(f32[3,16384]{1,0:T(4,128)} %offset_in.1) | copy-start | bytes 589828
  2.6 0.8 %copy-start.3 = (s32[16384]{0:T(1024)S(1)}, s32[16384]{0:T(1024)}, u32[]{:S(2)}) copy-start(s32[16384]{0:T(1024)} %param.8) | copy-start | bytes 196612
  3.5 0.8 %copy-start.4 = (s32[2,8192]{1,0:T(2,128)S(1)}, s32[2,8192]{1,0:T(2,128)}, u32[]{:S(2)}) copy-start(s32[2,8192]{1,0:T(2,128)} %rows_in.1) | copy-start | bytes 196612
  4.3 0.7 %copy-start.5 = (s32[256]{0:T(256)S(1)}, s32[256]{0:T(256)}, u32[]{:S(2)}) copy-start(s32[256]{0:T(256)} %bricks_in.1) | copy-start | bytes 3076
  21.2 5.5 %copy-start = (f32[5,4,64,256]{3,2,1,0:T(8,128)S(1)}, f32[5,4,64,256]{3,2,1,0:T(8,128)}, u32[]{:S(2)}) copy-start(f32[5,4,64,256]{3,2,1,0:T(8,128)} %gas.3) | copy-start | bytes 3932164

commit v4 on v3

--- a/solution.py
+++ b/solution.py
@@ -15,6 +15,8 @@
 GROUP = 6
 SPAN = 4 * GROUP
 NT = (((1,), (1,)), ((), ()))
+SMEM = pl.BlockSpec(memory_space=pltpu.SMEM)
+VMEM = pl.BlockSpec(memory_space=pltpu.VMEM)
 F32 = jnp.float32
 BF16 = jnp.bfloat16
 
@@ -32,25 +34,31 @@
     return lax.broadcasted_iota(jnp.int32, shape, 0)
 
 
+def clear_kernel(total, gone):
+    total[...] = jnp.zeros_like(total)
+    gone[...] = jnp.zeros_like(gone)
+
+
+def clear_call(grid, blocks):
+    return pl.pallas_call(
+        clear_kernel,
+        out_shape=(
+            jax.ShapeDtypeStruct((grid.rows, LANES), F32),
+            jax.ShapeDtypeStruct((blocks, LANES), F32),
+        ),
+        compiler_params=pltpu.CompilerParams(vmem_limit_bytes=2**20),
+        cost_estimate=pl.CostEstimate(
+            flops=10**10, bytes_accessed=2 * 10**6, transcendentals=0
+        ),
+        name="clear",
+    )()
+
+
 def gather_kernel(
-    load_in, offset_in, cell_in, rows_in, bricks_in, up, down, stay, bricks, load, offset,
-    cell, rows, table, base, corner, gone, arrived
+    load, offset, cell, rows, none_gone, up, down, stay, table, base, corner, gone
 ):
-    pairs = (
-        (cell_in, cell), (load_in, load), (offset_in, offset), (rows_in, rows),
-        (bricks_in, bricks),
-    )
-    copies = [
-        pltpu.make_async_copy(source, target, arrived.at[i])
-        for i, (source, target) in enumerate(pairs)
-    ]
-    for each in copies:
-        each.start()
-    for each in copies:
-        each.wait()
     count = load.shape[1]
     blocks = count // LANES
-    slots = rows.shape[1]
     axis_row = row_numbers((3, count))
     coords = lax.shift_right_logical(
         jnp.broadcast_to(cell[...], (3, count)), 4 - 2 * axis_row
@@ -68,7 +76,7 @@
         return carry
 
     lax.fori_loop(0, blocks // 2, fill, 0, unroll=8)
-    gone[...] = jnp.zeros_like(gone)
+    gone[...] = none_gone[...]
 
     for side, out in ((0, up), (1, down)):
         out[...] = jnp.zeros_like(out)
@@ -111,33 +119,26 @@
     lax.fori_loop(0, blocks, keep, 0, unroll=8)
 
 
-def gather_call(load, offset, cell, rows, bricks):
+def gather_call(load, offset, cell, rows, none_gone):
     count = load.shape[1]
     slots = rows.shape[1]
     moved = jax.ShapeDtypeStruct((8, slots), F32)
     return pl.pallas_call(
         gather_kernel,
-        out_shape=(
-            moved,
-            moved,
-            jax.ShapeDtypeStruct((8, count), F32),
-            jax.ShapeDtypeStruct(bricks.shape, jnp.int32),
-        ),
-        in_specs=[pl.BlockSpec(memory_space=pltpu.HBM)] * 5,
+        out_shape=(moved, moved, jax.ShapeDtypeStruct((8, count), F32)),
+        in_specs=[VMEM] * 5,
         scratch_shapes=[
-            pltpu.VMEM(load.shape, F32),
-            pltpu.VMEM(offset.shape, F32),
-            pltpu.VMEM((1, count), jnp.int32),
-            pltpu.VMEM(rows.shape, jnp.int32),
             pltpu.VMEM((8 * (count // LANES), 2 * LANES), BF16),
             pltpu.VMEM((8, count), F32),
             pltpu.VMEM((8, count), F32),
             pltpu.VMEM((count // LANES, LANES), F32),
-            pltpu.SemaphoreType.DMA((5,)),
         ],
         compiler_params=pltpu.CompilerParams(vmem_limit_bytes=16 * 2**20),
+        cost_estimate=pl.CostEstimate(
+            flops=10**10, bytes_accessed=2 * 10**6, transcendentals=0
+        ),
         name="gather_rows",
-    )(load, offset, cell.reshape(1, count), rows, bricks)
+    )(load, offset, cell.reshape(1, count), rows, none_gone)
 
 
 class Grid:
@@ -150,13 +151,15 @@
         self.rows_z = span_z + 8
         self.rows = self.groups * FIELDS * self.rows_z
         self.pad_y = self.groups * SPAN
+        self.shift = self.per_row.bit_length() - 1
+        assert self.per_row == 1 << self.shift and self.bricks_y & (self.bricks_y - 1) == 0
 
     def place(self, brick):
-        z = brick % self.per_row
-        y = (brick // self.per_row) % self.bricks_y
-        group = y // GROUP
+        z = brick & (self.per_row - 1)
+        y = lax.shift_right_logical(brick, self.shift) & (self.bricks_y - 1)
+        group = sum((y >= GROUP * k).astype(jnp.int32) for k in range(1, self.groups))
         first = group * (FIELDS * self.rows_z) + 4 * z
-        return first, (4 * (y - group * GROUP)).astype(F32)
+        return first, (4 * y - SPAN * group).astype(F32)
 
 
 def plane_weights(block, shift_y):
@@ -212,11 +215,12 @@
     )
 
 
-UNROLL = 32
-
-
-def deposit_kernel(grid, bricks, spread, lower, upper, total):
-    total[...] = jnp.zeros_like(total)
+UNROLL = 64
+TURN = 32
+
+
+def deposit_kernel(grid, bricks, spread, lower, upper, zeros, total):
+    del zeros
     blocks = lower.shape[1] // LANES
     resident = bricks.shape[0] - 2 * blocks
     ratio = resident // (2 * blocks)
@@ -267,9 +271,8 @@
 
 def fill_faces(grid, f, second_half, gas, sums, up, down, row):
     ny = grid.span_y
-    up[f] = sums[f, 4]
-    down[f, :ny] = COUPLE * sums[f, 0, :ny] + gas[f, 0]
-    down[f, ny:] = COUPLE * sums[f, 0, ny:]
+    up[f] = sums[f, 4, :ny]
+    down[f] = COUPLE * sums[f, 0, :ny] + gas[f, 0]
     for x in range(5):
         low_row = COUPLE * sums[f, x, 0:1, :]
         if x < 4:
@@ -280,7 +283,7 @@
 
 def sample_kernel(
     grid, last, bricks, stay, lower, upper, gas, sums, from_up, from_down,
-    from_row, corner_low, corner_high, weights, source, sampled, field, held
+    from_row, corner_low, corner_high, tail_low, tail_high, weights, source, sampled, field, held
 ):
     ny = grid.span_y
     second_half = lax.axis_index("radial") == 1
@@ -297,18 +300,18 @@
             head = jnp.where(first, 2.0 * face * extra, 0.0)
             mine = sums[f, x, :ny, :]
             if x == 0:
-                mine = mine + from_up[f, :ny, :]
+                mine = mine + from_up[f]
             mine = jnp.concatenate([mine[:8] + head, mine[8:]], 0)
             tail = COUPLE * sums[f, x, ny : ny + 8, :]
             if x == 0:
-                tail = tail + COUPLE * from_up[f, ny : ny + 8, :]
+                tail = tail + tail_low[f : f + 1, :]
             if x < 4:
                 source[f, x] = mine
                 mine = gas[f, x] + COUPLE * mine
             else:
-                mine = COUPLE * mine + from_down[f, :ny, :]
+                mine = COUPLE * mine + from_down[f]
                 mine = jnp.where(at_end, 0.0, mine)
-                tail = tail + from_down[f, ny : ny + 8, :]
+                tail = tail + tail_high[f : f + 1, :]
                 tail = jnp.where(at_end, 0.0, tail)
                 extra = jnp.where(at_end, 0.0, extra)
             tail = jnp.where(first & jnp.logical_not(second_half), tail + extra, 0.0)
@@ -347,21 +350,18 @@
         offset += blocks
 
 
-SMEM = pl.BlockSpec(memory_space=pltpu.SMEM)
-VMEM = pl.BlockSpec(memory_space=pltpu.VMEM)
-
-
 BIG = pltpu.CompilerParams(vmem_limit_bytes=12 * 2**20)
 
 
-def deposit_call(grid, bricks, spread, lower, upper):
+def deposit_call(grid, bricks, spread, lower, upper, zeros):
     return pl.pallas_call(
         functools.partial(deposit_kernel, grid),
         out_shape=jax.ShapeDtypeStruct((grid.rows, LANES), F32),
-        in_specs=[SMEM, VMEM, VMEM, VMEM],
+        in_specs=[SMEM, VMEM, VMEM, VMEM, VMEM],
+        input_output_aliases={4: 0},
         compiler_params=BIG,
         name="deposit",
-    )(bricks, spread, lower, upper)
+    )(bricks, spread, lower, upper, zeros)
 
 
 def signal_entry(axial_at, radial_at):
@@ -406,8 +406,8 @@
     falling = copy(1, down, upper, a - 1)
 
     def step(turn, carry):
-        for i in range(UNROLL):
-            at = turn * UNROLL + i
+        for i in range(TURN):
+            at = turn * TURN + i
             block = stay[:, pl.ds(pl.multiple_of(at * LANES, LANES), LANES)]
             plane = plane_weights(block, grid.place(bricks[at])[1])
             rows = pl.ds(pl.multiple_of(at * 8 * FIELDS, 8), 8 * FIELDS)
@@ -434,7 +434,7 @@
     def _():
         upper[...] = jnp.zeros_like(upper)
 
-    lax.fori_loop(FILLER, stay.shape[1] // LANES // UNROLL, step, 0)
+    lax.fori_loop(FILLER, stay.shape[1] // LANES // TURN, step, 0)
 
     @pl.when(has_above)
     def _():
@@ -468,7 +468,7 @@
 
 def exchange_kernel(
     grid, last, bricks, stay, lower, upper, gas, total, sums, from_up, from_down, from_row,
-    corner_low, corner_high, weights, up, down, edge, sent, got
+    corner_low, corner_high, tail_low, tail_high, weights, up, down, edge, sent, got
 ):
     a = lax.axis_index("axial")
     r = lax.axis_index("radial")
@@ -496,60 +496,73 @@
         )
 
     row = copy(0, edge, from_row, a, 1 - r)
-    corner_up = copy(1, edge.at[4], corner_low, a + 1, 1 - r)
-    corner_down = copy(2, edge.at[0], corner_high, a - 1, 1 - r)
-    faces_up = [copy(3 + f, up.at[f], from_up.at[f], a + 1, r) for f in range(FIELDS)]
+    ends_up = [
+        copy(1, edge.at[4], corner_low, a + 1, 1 - r),
+        copy(2, edge.at[4], tail_low, a + 1, r),
+    ]
+    ends_down = [
+        copy(3, edge.at[0], corner_high, a - 1, 1 - r),
+        copy(4, edge.at[0], tail_high, a - 1, r),
+    ]
+    faces_up = [copy(5 + f, up.at[f], from_up.at[f], a + 1, r) for f in range(FIELDS)]
     faces_down = [
-        copy(3 + FIELDS + f, down.at[f], from_down.at[f], a - 1, r) for f in range(FIELDS)
+        copy(5 + FIELDS + f, down.at[f], from_down.at[f], a - 1, r) for f in range(FIELDS)
     ]
     select = merge_selector()
     for x in range(5):
         edge[x, FIELDS:, :] = jnp.zeros((8 - FIELDS, grid.span_z), F32)
     def weigh(part, offset):
         def step(turn, carry):
-            for i in range(UNROLL):
-                at = turn * UNROLL + i
+            for i in range(TURN):
+                at = turn * TURN + i
                 block = part[:, pl.ds(pl.multiple_of(at * LANES, LANES), LANES)]
                 plane = plane_weights(block, grid.place(bricks[offset + at])[1])
                 store_weights(weights, offset + at, plane)
             return carry
 
-        lax.fori_loop(0, part.shape[1] // LANES // UNROLL, step, 0)
+        lax.fori_loop(0, part.shape[1] // LANES // TURN, step, 0)
 
     for f in range(FIELDS):
         merge_field(grid, f, select, total, sums)
         fill_faces(grid, f, r == 1, gas, sums, up, down, edge)
     weigh(stay, 0)
     pl.semaphore_wait(pltpu.get_barrier_semaphore(), peers)
-    for f in range(FIELDS):
-
-        @pl.when(has_above)
-        def _(f=f):
-            faces_up[f].start()
-
-        @pl.when(has_below)
-        def _(f=f):
-            faces_down[f].start()
-
     row.start()
 
     @pl.when(has_above)
     def _():
-        corner_up.start()
+        for each in ends_up:
+            each.start()
 
     @pl.when(has_below)
     def _():
-        corner_down.start()
+        for each in ends_down:
+            each.start()
+
+    upper_core = a % 2 == 1
+    for far in (True, False):
+
+        @pl.when(has_above & (upper_core == far))
+        def _():
+            for each in faces_up:
+                each.start()
+
+        @pl.when(has_below & (upper_core != far))
+        def _():
+            for each in faces_down:
+                each.start()
 
     @pl.when(jnp.logical_not(has_below))
     def _():
         from_up[...] = jnp.zeros_like(from_up)
         corner_low[...] = jnp.zeros_like(corner_low)
+        tail_low[...] = jnp.zeros_like(tail_low)
 
     @pl.when(jnp.logical_not(has_above))
     def _():
         from_down[...] = jnp.zeros_like(from_down)
         corner_high[...] = jnp.zeros_like(corner_high)
+        tail_high[...] = jnp.zeros_like(tail_high)
 
     resident = stay.shape[1] // LANES
     weigh(lower, resident)
@@ -558,24 +571,24 @@
 
     @pl.when(has_above)
     def _():
-        for each in faces_up + [corner_up]:
+        for each in faces_up + ends_up:
             each.wait_send()
-        for each in faces_down + [corner_down]:
+        for each in faces_down + ends_down:
             each.wait_recv()
 
     @pl.when(has_below)
     def _():
-        for each in faces_down + [corner_down]:
+        for each in faces_down + ends_down:
             each.wait_send()
-        for each in faces_up + [corner_up]:
+        for each in faces_up + ends_up:
             each.wait_recv()
 
 
 def exchange_call(grid, last, bricks, stay, lower, upper, gas, total):
-    plane = (FIELDS, grid.pad_y, grid.span_z)
+    plane = (FIELDS, grid.span_y, grid.span_z)
     edge = (5, 8, grid.span_z)
     corner = jax.ShapeDtypeStruct(edge[1:], F32)
-    copies = 3 + 2 * FIELDS
+    copies = 5 + 2 * FIELDS
     return pl.pallas_call(
         functools.partial(exchange_kernel, grid, last),
         out_shape=(
@@ -585,10 +598,12 @@
             jax.ShapeDtypeStruct(edge, F32),
             corner,
             corner,
+            corner,
+            corner,
             jax.ShapeDtypeStruct((bricks.shape[0] * 2 * LANES, LANES), BF16),
         ),
         in_specs=[SMEM] + [VMEM] * 5,
-        out_specs=(VMEM,) * 7,
+        out_specs=(VMEM,) * 9,
         scratch_shapes=[
             pltpu.VMEM(plane, F32),
             pltpu.VMEM(plane, F32),
@@ -611,7 +626,7 @@
             jax.ShapeDtypeStruct(gas.shape, F32),
             jax.ShapeDtypeStruct((FIELDS, bricks.shape[0] * LANES), BF16),
         ),
-        in_specs=[SMEM] + [VMEM] * 11,
+        in_specs=[SMEM] + [VMEM] * 13,
         scratch_shapes=[
             pltpu.VMEM((FIELDS, 5, grid.pad_y, grid.span_z), F32),
             pltpu.VMEM((grid.rows, LANES), F32),
@@ -625,9 +640,10 @@
     axial = lax.axis_size("axial")
     span_y, span_z = gas.shape[2], gas.shape[3]
     grid = Grid(span_y, span_z)
-    up, down, stay, bricks = gather_call(load, offset, cell, rows, bricks)
+    zeros, none_gone = clear_call(grid, load.shape[1] // LANES)
+    up, down, stay = gather_call(load, offset, cell, rows, none_gone)
     lower, upper, spread = migrate_call(grid, axial - 1, bricks, up, down, stay)
-    total = deposit_call(grid, bricks, spread, lower, upper)
+    total = deposit_call(grid, bricks, spread, lower, upper, zeros)
     arrived = exchange_call(grid, axial - 1, bricks, stay, lower, upper, gas, total)
     return sample_call(
         grid, axial - 1, bricks, stay, lower, upper, gas, *arrived

time: 52.9 us -> 44.8 us (0.85); the launches traced: 52.1 us -> 44.7 us
  Pallas kernels: 47.1 us -> 43 us
  local copies, waits for them, and re-layouts: 4.35 us -> 0.95 us
    unnamed x12, local copies, waits for them, and re-layouts: 4.35 us -> 0.95 us
    pallas_call x1, Pallas kernels: 8 us -> 5.84 us  [sample_call(): pl.pallas_call(functools.partial(sample_kernel, grid, last), out_shape=(j...]
    pallas_call x1, Pallas kernels: 5.47 us -> 3.62 us  [deposit_call(): pl.pallas_call(functools.partial(deposit_kernel, grid), out_shape=jax.Sha...]
where the time goes in v4:
time: 44.8 us; the launch traced here: 44.7 us
  Pallas kernels  43 us (96%)
  local copies, waits for them, and re-layouts  0.95 us (2%)
  between operations  0.73 us (2%)
    pallas_call x1, Pallas kernels, exchange_call(): pl.pallas_call(functools.partial(exchange_kernel, grid, last), out_shape=...  17.4 us
    pallas_call x1, Pallas kernels, migrate_call(): pl.pallas_call(functools.partial(migrate_kernel, grid, last), out_shape=(...  12.1 us
    pallas_call x1, Pallas kernels, sample_call(): pl.pallas_call(functools.partial(sample_kernel, grid, last), out_shape=(j...  5.84 us
    pallas_call x1, Pallas kernels, gather_call(): pl.pallas_call(gather_kernel, out_shape=(moved, moved, jax.ShapeDtypeStru...  3.92 us
    pallas_call x1, Pallas kernels, deposit_call(): pl.pallas_call(functools.partial(deposit_kernel, grid), out_shape=jax.Sha...  3.62 us
    unnamed x12, local copies, waits for them, and re-layouts  0.95 us

profile of v4, /device:TPU:2, one launch (start us, length us, event | category | flops | bytes accessed | tf_op | source)
XLA Modules:
  0.0 44.7 jit_solution(6574433575449425645)
XLA Ops:
  0.6 0.0 copy-start.2
  0.6 0.0 copy-start.3
  0.7 0.0 copy-start.4
  0.7 0.0 copy-start.5
  0.7 0.1 clear.1
  0.8 0.9 %copy-done.2 = f32[5,16384]{1,0:T(8,128)S(1)} copy-done((f32[5,16384]{1,0:T(8,128)S(1)}, f32[5,16384]{1,0:T(8,128)}, u32[]{:S(2)}) %copy-start.2) | copy-done | bytes 327704
  1.7 0.1 copy-done.3
  1.7 0.0 copy-done.4
  1.7 0.0 copy-done.5
  1.7 0.0 copy-start.1
  1.7 3.9 %gather_rows.1 = (f32[8,8192]{1,0:T(8,128)S(1)}, f32[8,8192]{1,0:T(8,128)S(1)}, f32[8,16384]{1,0:T(8,128)S(1)}) custom-call(f32[5,16384]{1,0:T(8,128)S(1)} %copy-done.2, f32[3,16384]{1,0:T(4,128)S(1)} %copy-done.3, s32[1,16384]{1,0:T(1,128)S(1)} %bitcast.1, s32[2,8192]{1,0:T(2,128)S(1)} %copy-done.5, f32[128,128]{1,0:T(8,128)S(1)} %get-tuple-element.19.none_gone), custom_call_target="tpu_custom_call" | custom-call | flops 10000000000 | bytes 2000000 | tf_op jit(solution)/shard_map/gather_rows/pallas_call | solution.py:126
  5.7 0.0 copy-done.1
  5.7 12.1 %migrate.1 = (f32[8,8192]{1,0:T(8,128)S(1)}, f32[8,8192]{1,0:T(8,128)S(1)}, f32[5120,128]{1,0:T(8,128)S(1)}) custom-call(s32[256]{0:T(256)S(1)} %copy-done.1, f32[8,8192]{1,0:T(8,128)S(1)} %get-tuple-element.21.up, f32[8,8192]{1,0:T(8,128)S(1)} %get-tuple-element.22.down, f32[8,16384]{1,0:T(8,128)S(1)} %get-tuple-element.20.stay), custom_call_target="tpu_custom_call" | custom-call | tf_op jit(solution)/shard_map/migrate/pallas_call | solution.py:452
  17.8 0.0 copy-start
  17.8 3.6 %deposit.1.total = f32[3960,128]{1,0:T(8,128)S(1)} custom-call(s32[256]{0:T(256)S(1)} %copy-done.1, f32[5120,128]{1,0:T(8,128)S(1)} %get-tuple-element.25.spread, f32[8,8192]{1,0:T(8,128)S(1)} %get-tuple-element.23.lower, f32[8,8192]{1,0:T(8,128)S(1)} %get-tuple-element.24.upper, f32[3960,128]{1,0:T(8,128)S(1)} %get-tuple-element.26.zeros), custom_call_target="tpu_custom_call", output_to_operand_aliasing={{}: (4, {})} | custom-call | tf_op jit(solution)/shard_map/deposit/pallas_call | solution.py:357
  21.5 0.0 copy-done
  21.5 17.4 %exchange.1 = (f32[5,5,72,256]{3,2,1,0:T(8,128)S(1)}, f32[5,64,256]{2,1,0:T(8,128)S(1)}, f32[5,64,256]{2,1,0:T(8,128)S(1)}, f32[5,8,256]{2,1,0:T(8,128)S(1)}, f3...) custom-call(s32[256]{0:T(256)S(1)} %copy-done.1, ...), custom_call_target="tpu_custom_call" | custom-call | tf_op jit(solution)/shard_map/exchange/pallas_call | solution.py:592
  38.9 5.8 %sample.1 = (f32[5,4,64,256]{3,2,1,0:T(8,128)}, bf16[5,32768]{1,0:T(8,128)(2,1)}) custom-call(s32[256]{0:T(256)S(1)} %copy-done.1, f32[8,16384]{1,0:T(8,128)S(1)} %get-tuple-element.20.stay, f32[8,8192]{1,0:T(8,128)S(1)} %get-tuple-element.23.lower, f32[8,8192]{1,0:T(8,128)S(1)} %get-tuple-element.24.upper, f32[5,4,64,256]{3,2,1,0:T(8,128)S(1)} %copy-done, ...), custom_call_target="tpu_custom_call" | custom-call | tf_op jit(solution)/shard_map/sample/pallas_call | solution.py:623
Async XLA Ops:
  0.6 1.0 %copy-start.2 = (f32[5,16384]{1,0:T(8,128)S(1)}, f32[5,16384]{1,0:T(8,128)}, u32[]{:S(2)}) copy-start(f32[5,16384]{1,0:T(8,128)} %load.1) | copy-start | bytes 983044
  0.6 1.1 %copy-start.3 = (f32[3,16384]{1,0:T(4,128)S(1)}, f32[3,16384]{1,0:T(4,128)}, u32[]{:S(2)}) copy-start(f32[3,16384]{1,0:T(4,128)} %offset.1) | copy-start | bytes 589828
  0.7 1.1 %copy-start.4 = (s32[16384]{0:T(1024)S(1)}, s32[16384]{0:T(1024)}, u32[]{:S(2)}) copy-start(s32[16384]{0:T(1024)} %param.8) | copy-start | bytes 196612
  0.7 1.1 %copy-start.5 = (s32[2,8192]{1,0:T(2,128)S(1)}, s32[2,8192]{1,0:T(2,128)}, u32[]{:S(2)}) copy-start(s32[2,8192]{1,0:T(2,128)} %rows.1) | copy-start | bytes 196612
  1.7 3.9 %copy-start.1 = (s32[256]{0:T(256)S(1)}, s32[256]{0:T(256)}, u32[]{:S(2)}) copy-start(s32[256]{0:T(256)} %bricks.7) | copy-start | bytes 3076
  17.8 3.6 %copy-start = (f32[5,4,64,256]{3,2,1,0:T(8,128)S(1)}, f32[5,4,64,256]{3,2,1,0:T(8,128)}, u32[]{:S(2)}) copy-start(f32[5,4,64,256]{3,2,1,0:T(8,128)} %gas.3) | copy-start | bytes 3932164

commit v5 on v4

--- a/solution.py
+++ b/solution.py
@@ -376,9 +376,6 @@
     target[pl.ds(place, 2 * LANES), :] = jnp.concatenate(weights, 0).astype(BF16)
 
 
-FILLER = 1
-
-
 def migrate_kernel(
     grid, last, bricks, up, down, stay, lower, upper, spread, sent, got
 ):
@@ -414,7 +411,6 @@
             spread[rows, :] = spread_block(block, plane)
         return carry
 
-    lax.fori_loop(0, FILLER, step, 0)
     peers = has_above.astype(jnp.int32) + has_below.astype(jnp.int32)
     pl.semaphore_wait(pltpu.get_barrier_semaphore(), peers)
 
@@ -434,7 +430,7 @@
     def _():
         upper[...] = jnp.zeros_like(upper)
 
-    lax.fori_loop(FILLER, stay.shape[1] // LANES // TURN, step, 0)
+    lax.fori_loop(0, stay.shape[1] // LANES // TURN, step, 0)
 
     @pl.when(has_above)
     def _():
@@ -525,7 +521,6 @@
     for f in range(FIELDS):
         merge_field(grid, f, select, total, sums)
         fill_faces(grid, f, r == 1, gas, sums, up, down, edge)
-    weigh(stay, 0)
     pl.semaphore_wait(pltpu.get_barrier_semaphore(), peers)
     row.start()
 
@@ -565,6 +560,7 @@
         tail_high[...] = jnp.zeros_like(tail_high)
 
     resident = stay.shape[1] // LANES
+    weigh(stay, 0)
     weigh(lower, resident)
     weigh(upper, resident + lower.shape[1] // LANES)
     row.wait()

time: 44.8 us -> 45.2 us (level)
    pallas_call x1, Pallas kernels: 17.4 us -> 18 us  [exchange_call(): pl.pallas_call(functools.partial(exchange_kernel, grid, last), out_shape=...]
where the time goes in v5:
time: 45.2 us; the launch traced here: 45.1 us
  Pallas kernels  43.4 us (96%)
  local copies, waits for them, and re-layouts  0.95 us (2%)
  between operations  0.73 us (2%)
    pallas_call x1, Pallas kernels, exchange_call(): pl.pallas_call(functools.partial(exchange_kernel, grid, last), out_shape=...  18 us
    pallas_call x1, Pallas kernels, migrate_call(): pl.pallas_call(functools.partial(migrate_kernel, grid, last), out_shape=(...  12 us
    pallas_call x1, Pallas kernels, sample_call(): pl.pallas_call(functools.partial(sample_kernel, grid, last), out_shape=(j...  5.83 us
    pallas_call x1, Pallas kernels, gather_call(): pl.pallas_call(gather_kernel, out_shape=(moved, moved, jax.ShapeDtypeStru...  3.92 us
    pallas_call x1, Pallas kernels, deposit_call(): pl.pallas_call(functools.partial(deposit_kernel, grid), out_shape=jax.Sha...  3.63 us
    unnamed x12, local copies, waits for them, and re-layouts  0.95 us

profile of v5, /device:TPU:2, one launch (start us, length us, event | category | flops | bytes accessed | tf_op | source)
XLA Modules:
  0.0 45.1 jit_solution(1105955376487420964)
XLA Ops:
  0.6 0.0 copy-start.2
  0.6 0.0 copy-start.3
  0.7 0.0 copy-start.4
  0.7 0.0 copy-start.5
  0.7 0.1 clear.1
  0.8 0.9 %copy-done.2 = f32[5,16384]{1,0:T(8,128)S(1)} copy-done((f32[5,16384]{1,0:T(8,128)S(1)}, f32[5,16384]{1,0:T(8,128)}, u32[]{:S(2)}) %copy-start.2) | copy-done | bytes 327704
  1.7 0.1 copy-done.3
  1.7 0.0 copy-done.4
  1.7 0.0 copy-done.5
  1.7 0.0 copy-start.1
  1.7 3.9 %gather_rows.1 = (f32[8,8192]{1,0:T(8,128)S(1)}, f32[8,8192]{1,0:T(8,128)S(1)}, f32[8,16384]{1,0:T(8,128)S(1)}) custom-call(f32[5,16384]{1,0:T(8,128)S(1)} %copy-done.2, f32[3,16384]{1,0:T(4,128)S(1)} %copy-done.3, s32[1,16384]{1,0:T(1,128)S(1)} %bitcast.1, s32[2,8192]{1,0:T(2,128)S(1)} %copy-done.5, f32[128,128]{1,0:T(8,128)S(1)} %get-tuple-element.19.none_gone), custom_call_target="tpu_custom_call" | custom-call | flops 10000000000 | bytes 2000000 | tf_op jit(solution)/shard_map/gather_rows/pallas_call | solution.py:126
  5.7 0.0 copy-done.1
  5.7 12.0 %migrate.1 = (f32[8,8192]{1,0:T(8,128)S(1)}, f32[8,8192]{1,0:T(8,128)S(1)}, f32[5120,128]{1,0:T(8,128)S(1)}) custom-call(s32[256]{0:T(256)S(1)} %copy-done.1, f32[8,8192]{1,0:T(8,128)S(1)} %get-tuple-element.21.up, f32[8,8192]{1,0:T(8,128)S(1)} %get-tuple-element.22.down, f32[8,16384]{1,0:T(8,128)S(1)} %get-tuple-element.20.stay), custom_call_target="tpu_custom_call" | custom-call | tf_op jit(solution)/shard_map/migrate/pallas_call | solution.py:448
  17.6 0.0 copy-start
  17.7 3.6 %deposit.1.total = f32[3960,128]{1,0:T(8,128)S(1)} custom-call(s32[256]{0:T(256)S(1)} %copy-done.1, f32[5120,128]{1,0:T(8,128)S(1)} %get-tuple-element.25.spread, f32[8,8192]{1,0:T(8,128)S(1)} %get-tuple-element.23.lower, f32[8,8192]{1,0:T(8,128)S(1)} %get-tuple-element.24.upper, f32[3960,128]{1,0:T(8,128)S(1)} %get-tuple-element.26.zeros), custom_call_target="tpu_custom_call", output_to_operand_aliasing={{}: (4, {})} | custom-call | tf_op jit(solution)/shard_map/deposit/pallas_call | solution.py:357
  21.3 0.0 copy-done
  21.3 18.0 %exchange.1 = (f32[5,5,72,256]{3,2,1,0:T(8,128)S(1)}, f32[5,64,256]{2,1,0:T(8,128)S(1)}, f32[5,64,256]{2,1,0:T(8,128)S(1)}, f32[5,8,256]{2,1,0:T(8,128)S(1)}, f3...) custom-call(s32[256]{0:T(256)S(1)} %copy-done.1, ...), custom_call_target="tpu_custom_call" | custom-call | tf_op jit(solution)/shard_map/exchange/pallas_call | solution.py:588
  39.3 5.8 %sample.1 = (f32[5,4,64,256]{3,2,1,0:T(8,128)}, bf16[5,32768]{1,0:T(8,128)(2,1)}) custom-call(s32[256]{0:T(256)S(1)} %copy-done.1, f32[8,16384]{1,0:T(8,128)S(1)} %get-tuple-element.20.stay, f32[8,8192]{1,0:T(8,128)S(1)} %get-tuple-element.23.lower, f32[8,8192]{1,0:T(8,128)S(1)} %get-tuple-element.24.upper, f32[5,4,64,256]{3,2,1,0:T(8,128)S(1)} %copy-done, ...), custom_call_target="tpu_custom_call" | custom-call | tf_op jit(solution)/shard_map/sample/pallas_call | solution.py:619
Async XLA Ops:
  0.6 1.0 %copy-start.2 = (f32[5,16384]{1,0:T(8,128)S(1)}, f32[5,16384]{1,0:T(8,128)}, u32[]{:S(2)}) copy-start(f32[5,16384]{1,0:T(8,128)} %load.1) | copy-start | bytes 983044
  0.6 1.1 %copy-start.3 = (f32[3,16384]{1,0:T(4,128)S(1)}, f32[3,16384]{1,0:T(4,128)}, u32[]{:S(2)}) copy-start(f32[3,16384]{1,0:T(4,128)} %offset.1) | copy-start | bytes 589828
  0.7 1.1 %copy-start.4 = (s32[16384]{0:T(1024)S(1)}, s32[16384]{0:T(1024)}, u32[]{:S(2)}) copy-start(s32[16384]{0:T(1024)} %param.8) | copy-start | bytes 196612
  0.7 1.1 %copy-start.5 = (s32[2,8192]{1,0:T(2,128)S(1)}, s32[2,8192]{1,0:T(2,128)}, u32[]{:S(2)}) copy-start(s32[2,8192]{1,0:T(2,128)} %rows.1) | copy-start | bytes 196612
  1.7 3.9 %copy-start.1 = (s32[256]{0:T(256)S(1)}, s32[256]{0:T(256)}, u32[]{:S(2)}) copy-start(s32[256]{0:T(256)} %bricks.7) | copy-start | bytes 3076
  17.6 3.7 %copy-start = (f32[5,4,64,256]{3,2,1,0:T(8,128)S(1)}, f32[5,4,64,256]{3,2,1,0:T(8,128)}, u32[]{:S(2)}) copy-start(f32[5,4,64,256]{3,2,1,0:T(8,128)} %gas.3) | copy-start | bytes 3932164

commit v6 on v5

--- a/solution.py
+++ b/solution.py
@@ -10,7 +10,8 @@
 COUPLE = 0.5
 LANES = 128
 TILE = 2048
-CHUNK = 32
+MATRIX_BLOCKS = 80
+CHUNK = 16
 FIELDS = 5
 GROUP = 6
 SPAN = 4 * GROUP
@@ -55,7 +56,8 @@
 
 
 def gather_kernel(
-    load, offset, cell, rows, none_gone, up, down, stay, table, base, corner, gone
+    load, offset, cell, rows, none_gone, up, down, stay, table, base, corner, gone,
+    attributes
 ):
     count = load.shape[1]
     blocks = count // LANES
@@ -65,6 +67,7 @@
     ) & 3
     corner[...] = jnp.concatenate([jnp.zeros((5, count), F32), coords.astype(F32)], 0)
     base[...] = jnp.concatenate([load[...], offset[...]], 0)
+    attributes[...] = base[...] + corner[...]
 
     def fill(step, carry):
         at = pl.multiple_of(step * 2 * LANES, 2 * LANES)
@@ -93,8 +96,12 @@
             gone[...] += lax.dot_general(block_hot, lane_hot, NT, preferred_element_type=F32)
             wanted = jnp.concatenate([lane_hot, lane_hot], 0)
             block8 = jnp.broadcast_to(block, (8, TILE))
+            lane8 = jnp.broadcast_to(lane, (8, TILE))
             found = jnp.zeros((8, TILE), F32)
-            for chunk in range(blocks // CHUNK):
+            pieces = []
+            chunks = MATRIX_BLOCKS // CHUNK
+            columns = TILE // LANES
+            for chunk in range(chunks):
                 part = jnp.dot(
                     table[8 * CHUNK * chunk : 8 * CHUNK * (chunk + 1), :], wanted,
                     preferred_element_type=F32,
@@ -103,6 +110,20 @@
                     found = jnp.where(
                         block8 == chunk * CHUNK + i, part[8 * i : 8 * i + 8, :], found
                     )
+                for j in range(columns * chunk // chunks, columns * (chunk + 1) // chunks):
+                    column = slice(LANES * j, LANES * (j + 1))
+                    piece = jnp.zeros((8, LANES), F32)
+                    for i in range(MATRIX_BLOCKS, blocks):
+                        taken = jnp.take_along_axis(
+                            attributes[:, i * LANES : (i + 1) * LANES], lane8[:, column],
+                            axis=1, mode="promise_in_bounds",
+                        )
+                        piece = jnp.where(block8[:, column] == i, taken, piece)
+                    pieces.append(piece)
+            if pieces and MATRIX_BLOCKS < blocks:
+                found = jnp.where(
+                    block8 < MATRIX_BLOCKS, found, jnp.concatenate(pieces, 1)
+                )
             out[:, pl.ds(at, TILE)] = found
             return carry
 
@@ -132,6 +153,7 @@
             pltpu.VMEM((8, count), F32),
             pltpu.VMEM((8, count), F32),
             pltpu.VMEM((count // LANES, LANES), F32),
+            pltpu.VMEM((8, count), F32),
         ],
         compiler_params=pltpu.CompilerParams(vmem_limit_bytes=16 * 2**20),
         cost_estimate=pl.CostEstimate(

time: 45.2 us -> 45 us (level)
    pallas_call x1, Pallas kernels: 3.92 us -> 3.32 us  [gather_call(): pl.pallas_call(gather_kernel, out_shape=(moved, moved, jax.ShapeDtypeStru...]
where the time goes in v6:
time: 45 us; the launch traced here: 44.9 us
  Pallas kernels  43.2 us (96%)
  local copies, waits for them, and re-layouts  0.95 us (2%)
  between operations  0.73 us (2%)
    pallas_call x1, Pallas kernels, exchange_call(): pl.pallas_call(functools.partial(exchange_kernel, grid, last), out_shape=...  18.3 us
    pallas_call x1, Pallas kernels, migrate_call(): pl.pallas_call(functools.partial(migrate_kernel, grid, last), out_shape=(...  12 us
    pallas_call x1, Pallas kernels, sample_call(): pl.pallas_call(functools.partial(sample_kernel, grid, last), out_shape=(j...  5.87 us
    pallas_call x1, Pallas kernels, deposit_call(): pl.pallas_call(functools.partial(deposit_kernel, grid), out_shape=jax.Sha...  3.63 us
    pallas_call x1, Pallas kernels, gather_call(): pl.pallas_call(gather_kernel, out_shape=(moved, moved, jax.ShapeDtypeStru...  3.32 us
    unnamed x12, local copies, waits for them, and re-layouts  0.95 us

profile of v6, /device:TPU:2, one launch (start us, length us, event | category | flops | bytes accessed | tf_op | source)
XLA Modules:
  0.0 44.9 jit_solution(5442272236778915901)
XLA Ops:
  0.6 0.0 copy-start.2
  0.6 0.0 copy-start.3
  0.7 0.0 copy-start.4
  0.7 0.0 copy-start.5
  0.7 0.1 clear.1
  0.8 0.9 %copy-done.2 = f32[5,16384]{1,0:T(8,128)S(1)} copy-done((f32[5,16384]{1,0:T(8,128)S(1)}, f32[5,16384]{1,0:T(8,128)}, u32[]{:S(2)}) %copy-start.2) | copy-done | bytes 327704
  1.7 0.1 copy-done.3
  1.7 0.0 copy-done.4
  1.7 0.0 copy-done.5
  1.7 0.0 copy-start.1
  1.7 3.3 %gather_rows.1 = (f32[8,8192]{1,0:T(8,128)S(1)}, f32[8,8192]{1,0:T(8,128)S(1)}, f32[8,16384]{1,0:T(8,128)S(1)}) custom-call(f32[5,16384]{1,0:T(8,128)S(1)} %copy-done.2, f32[3,16384]{1,0:T(4,128)S(1)} %copy-done.3, s32[1,16384]{1,0:T(1,128)S(1)} %bitcast.1, s32[2,8192]{1,0:T(2,128)S(1)} %copy-done.5, f32[128,128]{1,0:T(8,128)S(1)} %get-tuple-element.19.none_gone), custom_call_target="tpu_custom_call" | custom-call | flops 10000000000 | bytes 2000000 | tf_op jit(solution)/shard_map/gather_rows/pallas_call | solution.py:147
  5.1 0.0 copy-done.1
  5.1 12.0 %migrate.1 = (f32[8,8192]{1,0:T(8,128)S(1)}, f32[8,8192]{1,0:T(8,128)S(1)}, f32[5120,128]{1,0:T(8,128)S(1)}) custom-call(s32[256]{0:T(256)S(1)} %copy-done.1, f32[8,8192]{1,0:T(8,128)S(1)} %get-tuple-element.21.up, f32[8,8192]{1,0:T(8,128)S(1)} %get-tuple-element.22.down, f32[8,16384]{1,0:T(8,128)S(1)} %get-tuple-element.20.stay), custom_call_target="tpu_custom_call" | custom-call | tf_op jit(solution)/shard_map/migrate/pallas_call | solution.py:470
  17.0 0.0 copy-start
  17.1 3.6 %deposit.1.total = f32[3960,128]{1,0:T(8,128)S(1)} custom-call(s32[256]{0:T(256)S(1)} %copy-done.1, f32[5120,128]{1,0:T(8,128)S(1)} %get-tuple-element.25.spread, f32[8,8192]{1,0:T(8,128)S(1)} %get-tuple-element.23.lower, f32[8,8192]{1,0:T(8,128)S(1)} %get-tuple-element.24.upper, f32[3960,128]{1,0:T(8,128)S(1)} %get-tuple-element.26.zeros), custom_call_target="tpu_custom_call", output_to_operand_aliasing={{}: (4, {})} | custom-call | tf_op jit(solution)/shard_map/deposit/pallas_call | solution.py:379
  20.7 0.0 copy-done
  20.7 18.3 %exchange.1 = (f32[5,5,72,256]{3,2,1,0:T(8,128)S(1)}, f32[5,64,256]{2,1,0:T(8,128)S(1)}, f32[5,64,256]{2,1,0:T(8,128)S(1)}, f32[5,8,256]{2,1,0:T(8,128)S(1)}, f3...) custom-call(s32[256]{0:T(256)S(1)} %copy-done.1, ...), custom_call_target="tpu_custom_call" | custom-call | tf_op jit(solution)/shard_map/exchange/pallas_call | solution.py:610
  39.0 5.9 %sample.1 = (f32[5,4,64,256]{3,2,1,0:T(8,128)}, bf16[5,32768]{1,0:T(8,128)(2,1)}) custom-call(s32[256]{0:T(256)S(1)} %copy-done.1, f32[8,16384]{1,0:T(8,128)S(1)} %get-tuple-element.20.stay, f32[8,8192]{1,0:T(8,128)S(1)} %get-tuple-element.23.lower, f32[8,8192]{1,0:T(8,128)S(1)} %get-tuple-element.24.upper, f32[5,4,64,256]{3,2,1,0:T(8,128)S(1)} %copy-done, ...), custom_call_target="tpu_custom_call" | custom-call | tf_op jit(solution)/shard_map/sample/pallas_call | solution.py:641
Async XLA Ops:
  0.6 1.0 %copy-start.2 = (f32[5,16384]{1,0:T(8,128)S(1)}, f32[5,16384]{1,0:T(8,128)}, u32[]{:S(2)}) copy-start(f32[5,16384]{1,0:T(8,128)} %load.1) | copy-start | bytes 983044
  0.6 1.1 %copy-start.3 = (f32[3,16384]{1,0:T(4,128)S(1)}, f32[3,16384]{1,0:T(4,128)}, u32[]{:S(2)}) copy-start(f32[3,16384]{1,0:T(4,128)} %offset.1) | copy-start | bytes 589828
  0.7 1.1 %copy-start.4 = (s32[16384]{0:T(1024)S(1)}, s32[16384]{0:T(1024)}, u32[]{:S(2)}) copy-start(s32[16384]{0:T(1024)} %param.8) | copy-start | bytes 196612
  0.7 1.1 %copy-start.5 = (s32[2,8192]{1,0:T(2,128)S(1)}, s32[2,8192]{1,0:T(2,128)}, u32[]{:S(2)}) copy-start(s32[2,8192]{1,0:T(2,128)} %rows.1) | copy-start | bytes 196612
  1.7 3.3 %copy-start.1 = (s32[256]{0:T(256)S(1)}, s32[256]{0:T(256)}, u32[]{:S(2)}) copy-start(s32[256]{0:T(256)} %bricks.7) | copy-start | bytes 3076
  17.0 3.6 %copy-start = (f32[5,4,64,256]{3,2,1,0:T(8,128)S(1)}, f32[5,4,64,256]{3,2,1,0:T(8,128)}, u32[]{:S(2)}) copy-start(f32[5,4,64,256]{3,2,1,0:T(8,128)} %gas.3) | copy-start | bytes 3932164

commit v7 on v6

--- a/solution.py
+++ b/solution.py
@@ -238,6 +238,17 @@
 
 
 UNROLL = 64
+CHUNK_BLOCKS = 16
+
+
+def filled_chunks(part):
+    wide = CHUNK_BLOCKS * LANES
+    return [
+        (at // LANES, jnp.max(jnp.abs(part[:, at : at + wide])) > 0.0)
+        for at in range(0, part.shape[1], wide)
+    ]
+
+
 TURN = 32
 
 
@@ -247,21 +258,27 @@
     resident = bricks.shape[0] - 2 * blocks
     ratio = resident // (2 * blocks)
     for part, offset in ((lower, 0), (upper, blocks)):
-
-        def step(turn, carry, part=part, offset=offset):
-            for i in range(UNROLL):
-                at = turn * UNROLL + i
-                block = part[:, pl.ds(pl.multiple_of(at * LANES, LANES), LANES)]
-                brick = bricks[resident + offset + at]
-                weights = plane_weights(block, grid.place(brick)[1])
-                add_block(grid, spread_block(block, weights), brick, total)
+        for first, filled in filled_chunks(part):
+
+            def own_blocks(at, offset=offset):
                 for j in range(ratio):
                     own = (offset + at) * ratio + j
-                    rows = pl.ds(pl.multiple_of(own * 8 * FIELDS, 8), 8 * FIELDS)
+                    rows = pl.ds(own * 8 * FIELDS, 8 * FIELDS)
                     add_block(grid, spread[rows, :], bricks[own], total)
-            return carry
-
-        lax.fori_loop(0, blocks // UNROLL, step, 0)
+
+            @pl.when(filled)
+            def _(part=part, offset=offset, first=first, own_blocks=own_blocks):
+                for at in range(first, first + CHUNK_BLOCKS):
+                    block = part[:, at * LANES : (at + 1) * LANES]
+                    brick = bricks[resident + offset + at]
+                    weights = plane_weights(block, grid.place(brick)[1])
+                    add_block(grid, spread_block(block, weights), brick, total)
+                    own_blocks(at)
+
+            @pl.when(jnp.logical_not(filled))
+            def _(first=first, own_blocks=own_blocks):
+                for at in range(first, first + CHUNK_BLOCKS):
+                    own_blocks(at)
 
 
 def merge_selector():

time: 45 us -> 43.2 us (0.960)
  Pallas kernels: 43.2 us -> 41.3 us
    pallas_call x1, Pallas kernels: 3.63 us -> 2.42 us  [deposit_call(): pl.pallas_call(functools.partial(deposit_kernel, grid), out_shape=jax.Sha...]
    pallas_call x1, Pallas kernels: 18.3 us -> 17.7 us  [exchange_call(): pl.pallas_call(functools.partial(exchange_kernel, grid, last), out_shape=...]
where the time goes in v7:
time: 43.2 us; the launch traced here: 43 us
  Pallas kernels  41.3 us (96%)
  local copies, waits for them, and re-layouts  0.95 us (2%)
  between operations  0.73 us (2%)
    pallas_call x1, Pallas kernels, exchange_call(): pl.pallas_call(functools.partial(exchange_kernel, grid, last), out_shape=...  17.7 us
    pallas_call x1, Pallas kernels, migrate_call(): pl.pallas_call(functools.partial(migrate_kernel, grid, last), out_shape=(...  12 us
    pallas_call x1, Pallas kernels, sample_call(): pl.pallas_call(functools.partial(sample_kernel, grid, last), out_shape=(j...  5.82 us
    pallas_call x1, Pallas kernels, gather_call(): pl.pallas_call(gather_kernel, out_shape=(moved, moved, jax.ShapeDtypeStru...  3.32 us
    pallas_call x1, Pallas kernels, deposit_call(): pl.pallas_call(functools.partial(deposit_kernel, grid), out_shape=jax.Sha...  2.42 us
    unnamed x12, local copies, waits for them, and re-layouts  0.95 us

profile of v7, /device:TPU:2, one launch (start us, length us, event | category | flops | bytes accessed | tf_op | source)
XLA Modules:
  0.0 43.0 jit_solution(14312187883235256165)
XLA Ops:
  0.6 0.0 copy-start.2
  0.6 0.0 copy-start.3
  0.7 0.0 copy-start.4
  0.7 0.0 copy-start.5
  0.7 0.1 clear.1
  0.8 0.9 %copy-done.2 = f32[5,16384]{1,0:T(8,128)S(1)} copy-done((f32[5,16384]{1,0:T(8,128)S(1)}, f32[5,16384]{1,0:T(8,128)}, u32[]{:S(2)}) %copy-start.2) | copy-done | bytes 327704
  1.7 0.1 copy-done.3
  1.7 0.0 copy-done.4
  1.7 0.0 copy-done.5
  1.7 0.0 copy-start.1
  1.7 3.3 %gather_rows.1 = (f32[8,8192]{1,0:T(8,128)S(1)}, f32[8,8192]{1,0:T(8,128)S(1)}, f32[8,16384]{1,0:T(8,128)S(1)}) custom-call(f32[5,16384]{1,0:T(8,128)S(1)} %copy-done.2, f32[3,16384]{1,0:T(4,128)S(1)} %copy-done.3, s32[1,16384]{1,0:T(1,128)S(1)} %bitcast.1, s32[2,8192]{1,0:T(2,128)S(1)} %copy-done.5, f32[128,128]{1,0:T(8,128)S(1)} %get-tuple-element.19.none_gone), custom_call_target="tpu_custom_call" | custom-call | flops 10000000000 | bytes 2000000 | tf_op jit(solution)/shard_map/gather_rows/pallas_call | solution.py:147
  5.1 0.0 copy-done.1
  5.1 12.0 %migrate.1 = (f32[8,8192]{1,0:T(8,128)S(1)}, f32[8,8192]{1,0:T(8,128)S(1)}, f32[5120,128]{1,0:T(8,128)S(1)}) custom-call(s32[256]{0:T(256)S(1)} %copy-done.1, f32[8,8192]{1,0:T(8,128)S(1)} %get-tuple-element.21.up, f32[8,8192]{1,0:T(8,128)S(1)} %get-tuple-element.22.down, f32[8,16384]{1,0:T(8,128)S(1)} %get-tuple-element.20.stay), custom_call_target="tpu_custom_call" | custom-call | tf_op jit(solution)/shard_map/migrate/pallas_call | solution.py:487
  17.0 0.0 copy-start
  17.1 2.4 %deposit.1.total = f32[3960,128]{1,0:T(8,128)S(1)} custom-call(s32[256]{0:T(256)S(1)} %copy-done.1, f32[5120,128]{1,0:T(8,128)S(1)} %get-tuple-element.25.spread, f32[8,8192]{1,0:T(8,128)S(1)} %get-tuple-element.23.lower, f32[8,8192]{1,0:T(8,128)S(1)} %get-tuple-element.24.upper, f32[3960,128]{1,0:T(8,128)S(1)} %get-tuple-element.26.zeros), custom_call_target="tpu_custom_call", output_to_operand_aliasing={{}: (4, {})} | custom-call | tf_op jit(solution)/shard_map/deposit/pallas_call | solution.py:396
  19.5 0.0 copy-done
  19.5 17.7 %exchange.1 = (f32[5,5,72,256]{3,2,1,0:T(8,128)S(1)}, f32[5,64,256]{2,1,0:T(8,128)S(1)}, f32[5,64,256]{2,1,0:T(8,128)S(1)}, f32[5,8,256]{2,1,0:T(8,128)S(1)}, f3...) custom-call(s32[256]{0:T(256)S(1)} %copy-done.1, ...), custom_call_target="tpu_custom_call" | custom-call | tf_op jit(solution)/shard_map/exchange/pallas_call | solution.py:627
  37.2 5.8 %sample.1 = (f32[5,4,64,256]{3,2,1,0:T(8,128)}, bf16[5,32768]{1,0:T(8,128)(2,1)}) custom-call(s32[256]{0:T(256)S(1)} %copy-done.1, f32[8,16384]{1,0:T(8,128)S(1)} %get-tuple-element.20.stay, f32[8,8192]{1,0:T(8,128)S(1)} %get-tuple-element.23.lower, f32[8,8192]{1,0:T(8,128)S(1)} %get-tuple-element.24.upper, f32[5,4,64,256]{3,2,1,0:T(8,128)S(1)} %copy-done, ...), custom_call_target="tpu_custom_call" | custom-call | tf_op jit(solution)/shard_map/sample/pallas_call | solution.py:658
Async XLA Ops:
  0.6 1.0 %copy-start.2 = (f32[5,16384]{1,0:T(8,128)S(1)}, f32[5,16384]{1,0:T(8,128)}, u32[]{:S(2)}) copy-start(f32[5,16384]{1,0:T(8,128)} %load.1) | copy-start | bytes 983044
  0.6 1.1 %copy-start.3 = (f32[3,16384]{1,0:T(4,128)S(1)}, f32[3,16384]{1,0:T(4,128)}, u32[]{:S(2)}) copy-start(f32[3,16384]{1,0:T(4,128)} %offset.1) | copy-start | bytes 589828
  0.7 1.1 %copy-start.4 = (s32[16384]{0:T(1024)S(1)}, s32[16384]{0:T(1024)}, u32[]{:S(2)}) copy-start(s32[16384]{0:T(1024)} %param.8) | copy-start | bytes 196612
  0.7 1.1 %copy-start.5 = (s32[2,8192]{1,0:T(2,128)S(1)}, s32[2,8192]{1,0:T(2,128)}, u32[]{:S(2)}) copy-start(s32[2,8192]{1,0:T(2,128)} %rows.1) | copy-start | bytes 196612
  1.7 3.3 %copy-start.1 = (s32[256]{0:T(256)S(1)}, s32[256]{0:T(256)}, u32[]{:S(2)}) copy-start(s32[256]{0:T(256)} %bricks.7) | copy-start | bytes 3076
  17.0 2.4 %copy-start = (f32[5,4,64,256]{3,2,1,0:T(8,128)S(1)}, f32[5,4,64,256]{3,2,1,0:T(8,128)}, u32[]{:S(2)}) copy-start(f32[5,4,64,256]{3,2,1,0:T(8,128)} %gas.3) | copy-start | bytes 3932164

commit v8 on v7

--- a/solution.py
+++ b/solution.py
@@ -453,13 +453,16 @@
     peers = has_above.astype(jnp.int32) + has_below.astype(jnp.int32)
     pl.semaphore_wait(pltpu.get_barrier_semaphore(), peers)
 
-    @pl.when(has_above)
-    def _():
-        rising.start()
-
-    @pl.when(has_below)
-    def _():
-        falling.start()
+    upper_core = a % 2 == 1
+    for far in (True, False):
+
+        @pl.when(has_above & (upper_core == far))
+        def _():
+            rising.start()
+
+        @pl.when(has_below & (upper_core != far))
+        def _():
+            falling.start()
 
     @pl.when(jnp.logical_not(has_below))
     def _():

time: 43.2 us -> 43.1 us (level)
  no operation moved by 1% of the time
where the time goes in v8:
time: 43.1 us; the launch traced here: 43 us
  Pallas kernels  41.4 us (96%)
  local copies, waits for them, and re-layouts  0.95 us (2%)
  between operations  0.72 us (2%)
    pallas_call x1, Pallas kernels, exchange_call(): pl.pallas_call(functools.partial(exchange_kernel, grid, last), out_shape=...  17.7 us
    pallas_call x1, Pallas kernels, migrate_call(): pl.pallas_call(functools.partial(migrate_kernel, grid, last), out_shape=(...  12 us
    pallas_call x1, Pallas kernels, sample_call(): pl.pallas_call(functools.partial(sample_kernel, grid, last), out_shape=(j...  5.85 us
    pallas_call x1, Pallas kernels, gather_call(): pl.pallas_call(gather_kernel, out_shape=(moved, moved, jax.ShapeDtypeStru...  3.32 us
    pallas_call x1, Pallas kernels, deposit_call(): pl.pallas_call(functools.partial(deposit_kernel, grid), out_shape=jax.Sha...  2.42 us
    unnamed x12, local copies, waits for them, and re-layouts  0.95 us

profile of v8, /device:TPU:2, one launch (start us, length us, event | category | flops | bytes accessed | tf_op | source)
XLA Modules:
  0.0 43.0 jit_solution(6544572778066326144)
XLA Ops:
  0.6 0.0 copy-start.2
  0.6 0.0 copy-start.3
  0.7 0.0 copy-start.4
  0.7 0.0 copy-start.5
  0.7 0.1 clear.1
  0.8 0.9 %copy-done.2 = f32[5,16384]{1,0:T(8,128)S(1)} copy-done((f32[5,16384]{1,0:T(8,128)S(1)}, f32[5,16384]{1,0:T(8,128)}, u32[]{:S(2)}) %copy-start.2) | copy-done | bytes 327704
  1.7 0.1 copy-done.3
  1.7 0.0 copy-done.4
  1.7 0.0 copy-done.5
  1.7 0.0 copy-start.1
  1.7 3.3 %gather_rows.1 = (f32[8,8192]{1,0:T(8,128)S(1)}, f32[8,8192]{1,0:T(8,128)S(1)}, f32[8,16384]{1,0:T(8,128)S(1)}) custom-call(f32[5,16384]{1,0:T(8,128)S(1)} %copy-done.2, f32[3,16384]{1,0:T(4,128)S(1)} %copy-done.3, s32[1,16384]{1,0:T(1,128)S(1)} %bitcast.1, s32[2,8192]{1,0:T(2,128)S(1)} %copy-done.5, f32[128,128]{1,0:T(8,128)S(1)} %get-tuple-element.19.none_gone), custom_call_target="tpu_custom_call" | custom-call | flops 10000000000 | bytes 2000000 | tf_op jit(solution)/shard_map/gather_rows/pallas_call | solution.py:147
  5.1 0.0 copy-done.1
  5.1 12.0 %migrate.1 = (f32[8,8192]{1,0:T(8,128)S(1)}, f32[8,8192]{1,0:T(8,128)S(1)}, f32[5120,128]{1,0:T(8,128)S(1)}) custom-call(s32[256]{0:T(256)S(1)} %copy-done.1, f32[8,8192]{1,0:T(8,128)S(1)} %get-tuple-element.21.up, f32[8,8192]{1,0:T(8,128)S(1)} %get-tuple-element.22.down, f32[8,16384]{1,0:T(8,128)S(1)} %get-tuple-element.20.stay), custom_call_target="tpu_custom_call" | custom-call | tf_op jit(solution)/shard_map/migrate/pallas_call | solution.py:490
  17.0 0.0 copy-start
  17.1 2.4 %deposit.1.total = f32[3960,128]{1,0:T(8,128)S(1)} custom-call(s32[256]{0:T(256)S(1)} %copy-done.1, f32[5120,128]{1,0:T(8,128)S(1)} %get-tuple-element.25.spread, f32[8,8192]{1,0:T(8,128)S(1)} %get-tuple-element.23.lower, f32[8,8192]{1,0:T(8,128)S(1)} %get-tuple-element.24.upper, f32[3960,128]{1,0:T(8,128)S(1)} %get-tuple-element.26.zeros), custom_call_target="tpu_custom_call", output_to_operand_aliasing={{}: (4, {})} | custom-call | tf_op jit(solution)/shard_map/deposit/pallas_call | solution.py:396
  19.5 0.0 copy-done
  19.5 17.7 %exchange.1 = (f32[5,5,72,256]{3,2,1,0:T(8,128)S(1)}, f32[5,64,256]{2,1,0:T(8,128)S(1)}, f32[5,64,256]{2,1,0:T(8,128)S(1)}, f32[5,8,256]{2,1,0:T(8,128)S(1)}, f3...) custom-call(s32[256]{0:T(256)S(1)} %copy-done.1, ...), custom_call_target="tpu_custom_call" | custom-call | tf_op jit(solution)/shard_map/exchange/pallas_call | solution.py:630
  37.2 5.8 %sample.1 = (f32[5,4,64,256]{3,2,1,0:T(8,128)}, bf16[5,32768]{1,0:T(8,128)(2,1)}) custom-call(s32[256]{0:T(256)S(1)} %copy-done.1, f32[8,16384]{1,0:T(8,128)S(1)} %get-tuple-element.20.stay, f32[8,8192]{1,0:T(8,128)S(1)} %get-tuple-element.23.lower, f32[8,8192]{1,0:T(8,128)S(1)} %get-tuple-element.24.upper, f32[5,4,64,256]{3,2,1,0:T(8,128)S(1)} %copy-done, ...), custom_call_target="tpu_custom_call" | custom-call | tf_op jit(solution)/shard_map/sample/pallas_call | solution.py:661
Async XLA Ops:
  0.6 1.0 %copy-start.2 = (f32[5,16384]{1,0:T(8,128)S(1)}, f32[5,16384]{1,0:T(8,128)}, u32[]{:S(2)}) copy-start(f32[5,16384]{1,0:T(8,128)} %load.1) | copy-start | bytes 983044
  0.6 1.1 %copy-start.3 = (f32[3,16384]{1,0:T(4,128)S(1)}, f32[3,16384]{1,0:T(4,128)}, u32[]{:S(2)}) copy-start(f32[3,16384]{1,0:T(4,128)} %offset.1) | copy-start | bytes 589828
  0.7 1.1 %copy-start.4 = (s32[16384]{0:T(1024)S(1)}, s32[16384]{0:T(1024)}, u32[]{:S(2)}) copy-start(s32[16384]{0:T(1024)} %param.8) | copy-start | bytes 196612
  0.7 1.1 %copy-start.5 = (s32[2,8192]{1,0:T(2,128)S(1)}, s32[2,8192]{1,0:T(2,128)}, u32[]{:S(2)}) copy-start(s32[2,8192]{1,0:T(2,128)} %rows.1) | copy-start | bytes 196612
  1.7 3.3 %copy-start.1 = (s32[256]{0:T(256)S(1)}, s32[256]{0:T(256)}, u32[]{:S(2)}) copy-start(s32[256]{0:T(256)} %bricks.7) | copy-start | bytes 3076
  17.0 2.4 %copy-start = (f32[5,4,64,256]{3,2,1,0:T(8,128)S(1)}, f32[5,4,64,256]{3,2,1,0:T(8,128)}, u32[]{:S(2)}) copy-start(f32[5,4,64,256]{3,2,1,0:T(8,128)} %gas.3) | copy-start | bytes 3932164
